TPU v7x, 256 devices: a whole 4x4x8 slice. The times are simulated.
256 devices in a mesh: ctx: 32 (over z, x), head: 4 (over y_hi, core), dp: 2 (over y_lo).
Axes of the slice: x: 4, y: 4 (y_hi: 2, y_lo: 2; y = y_hi * 2 + y_lo), z: 8, core: 2. Of those that a mesh axis runs over, the one named last changes fastest.
Arguments:
- queries: bfloat16 [8192, 32, 128], P(('dp', 'ctx'), 'head'), parts along dimension 0, may hold values from -6 to 6
- key_rows: bfloat16 [8192, 4, 128], P(('dp', 'ctx'), 'head'), parts along dimension 0, may hold values from -6 to 6
- value_rows: bfloat16 [8192, 4, 128], P(('dp', 'ctx'), 'head'), parts along dimension 0, may hold values from -6 to 6
- token_pos: int32 [8192], P(('dp', 'ctx')), parts along dimension 0, may hold values from 0 to 4095, as said below
- step_len: int32 [128], P('dp'), parts along dimension 0, may hold values from 1 to 512, 4096 in all
- label_count: int32 [128], P('dp'), parts along dimension 0, may hold values from 0 to 8
- out_grad: bfloat16 [8192, 32, 128], P(('dp', 'ctx'), 'head'), parts along dimension 0, may hold values from -8 to 8
- reward_weight: bfloat16 [32, 128], P('head'), may hold values from -1.25 to 1.25
Outputs:
- step_loss: float32 [128], P('dp'), parts along dimension 0
- d_query: bfloat16 [8192, 32, 128], P(('dp', 'ctx'), 'head'), parts along dimension 0
- d_key: bfloat16 [8192, 4, 128], P(('dp', 'ctx'), 'head'), parts along dimension 0
- d_value: bfloat16 [8192, 4, 128], P(('dp', 'ctx'), 'head'), parts along dimension 0
- d_reward: float32 [64, 128], P(('dp', 'head')), parts along dimension 0
There are 2 independent parts, one for each index of `dp`. A program takes and returns all parts, laid end to end along the dimension named above; an argument that names none is the same for every part. Nothing has to cross between parts.
Inputs may be any that keep to these rules, and one draw needn't show every extreme that they name: Each device's 128 rows of token_pos are two runs of 64 consecutive increasing positions, one beginning at c * 64 and the other at (63 - c) * 64 for a c of that device's own, in either order; over all 4096 rows every position appears once.
All inputs are finite; a program needn't handle non-finite values.
Results may differ from a plain program's by a relative error of at most 0.03.
Values may be sent and summed in bfloat16 or wider, within the bound.
A program may use at most 64 MiB of HBM per device.

v0:
```python
import math

import jax
import jax.numpy as jnp
from jax import lax
from jax.sharding import PartitionSpec as P

ROLLOUTS = 8


NEG_FILL = -1e30


def split_heads(block, groups):
    row_count, head_count, head_size = block.shape
    return block.reshape(row_count, groups, head_count // groups, head_size).transpose(1, 2, 0, 3)


def join_heads(block):
    groups, per_group, row_count, head_size = block.shape
    return block.transpose(2, 0, 1, 3).reshape(row_count, groups * per_group, head_size)


def score_block(query_split, key_block, score_scale):
    return (
        jnp.einsum("gjld,ngd->gjln", query_split, key_block, preferred_element_type=jnp.float32)
        * score_scale
    )


def attend(state, blocks, query_split, query_pos, score_scale):
    running_max, row_total, weighted = state
    key_block, value_block, key_pos = blocks
    visible = key_pos[None, :] <= query_pos[:, None]
    masked = jnp.where(visible, score_block(query_split, key_block, score_scale), NEG_FILL)
    new_max = jnp.maximum(running_max, jnp.max(masked, axis=-1))
    weights = jnp.where(visible, jnp.exp(masked - new_max[..., None]), 0.0)
    row_total = jnp.sum(weights, axis=-1)
    weighted = jnp.einsum(
        "gjln,ngd->gjld",
        weights.astype(jnp.bfloat16),
        value_block,
        preferred_element_type=jnp.float32,
    )
    return (new_max, row_total, weighted)


def back_block(blocks, query_split, query_pos, grad_split, log_total, delta_rows, score_scale):
    key_block, value_block, key_pos = blocks
    visible = key_pos[None, :] <= query_pos[:, None]
    shifted = jnp.where(
        visible, score_block(query_split, key_block, score_scale) - log_total[..., None], NEG_FILL
    )
    back_prob = jnp.exp(shifted)
    grad_prob = jnp.einsum(
        "gjld,ngd->gjln", grad_split, value_block, preferred_element_type=jnp.float32
    )
    grad_score = (back_prob * (grad_prob - delta_rows[..., None]) * score_scale).astype(
        jnp.bfloat16
    )
    query_term = jnp.einsum(
        "gjln,ngd->gjld", grad_score, key_block, preferred_element_type=jnp.float32
    )
    key_term = jnp.einsum(
        "gjln,gjld->ngd", grad_score, query_split, preferred_element_type=jnp.float32
    )
    value_term = jnp.einsum(
        "gjln,gjld->ngd",
        back_prob.astype(jnp.bfloat16),
        grad_split,
        preferred_element_type=jnp.float32,
    )
    return (query_term, key_term, value_term)


def local(queries, key_rows, value_rows, token_pos, step_len, label_count, out_grad, reward_weight):
    row_count, head_count, head_size = queries.shape
    groups = key_rows.shape[1]
    per_group = head_count // groups
    score_scale = 1.0 / math.sqrt(head_size)
    cycle_size = lax.axis_size("ctx")
    stride = math.gcd(cycle_size, max(1, 512 // row_count))
    block_count = cycle_size // stride
    whole_shape = (cycle_size * row_count,) + key_rows.shape[1:]
    query_split = split_heads(queries, groups)
    row_shape = (groups, per_group, row_count)
    empty = (
        jnp.full(row_shape, NEG_FILL, jnp.float32),
        jnp.zeros(row_shape, jnp.float32),
        jnp.zeros(row_shape + (head_size,), jnp.float32),
    )
    final_state = attend(
        empty,
        (
            lax.all_gather(key_rows, "ctx", axis=0, tiled=True),
            lax.all_gather(value_rows, "ctx", axis=0, tiled=True),
            lax.all_gather(token_pos, "ctx", axis=0, tiled=True),
        ),
        query_split,
        token_pos,
        score_scale,
    )
    running_max, row_total, weighted = final_state
    attended = (weighted / row_total[..., None]).astype(jnp.bfloat16)
    log_total = running_max + jnp.log(row_total)
    boundary = jnp.cumsum(step_len) - 1
    owned = (boundary[:, None] == token_pos[None, :]).astype(jnp.float32)
    weight_split = reward_weight.astype(jnp.float32).reshape(groups, per_group, head_size)
    attended_wide = attended.astype(jnp.float32)
    target = label_count.astype(jnp.float32) / ROLLOUTS
    row_score = jnp.sum(attended_wide * weight_split[:, :, None, :], axis=(0, 1, 3))
    logits = lax.psum(jnp.dot(owned, row_score, precision=lax.Precision.HIGHEST), ("ctx", "head"))
    misfit = jax.nn.sigmoid(logits) - target
    row_weight = jnp.dot(misfit, owned, precision=lax.Precision.HIGHEST)
    local_grad = jnp.einsum(
        "l,gjld->gjd", row_weight, attended_wide, precision=lax.Precision.HIGHEST
    )
    reward_grad = lax.psum(local_grad, "ctx")
    step_loss = jax.nn.softplus(logits) - target * logits
    grad_split = (
        split_heads(out_grad, groups).astype(jnp.float32)
        + row_weight[None, None, :, None] * weight_split[:, :, None, :]
    ).astype(jnp.bfloat16)
    delta_rows = jnp.sum(grad_split.astype(jnp.float32) * attended_wide, axis=-1)

    def back_terms(blocks):
        return back_block(
            blocks, query_split, token_pos, grad_split, log_total, delta_rows, score_scale
        )

    gathered = (
        lax.all_gather(key_rows, "ctx", axis=0, tiled=True),
        lax.all_gather(value_rows, "ctx", axis=0, tiled=True),
        lax.all_gather(token_pos, "ctx", axis=0, tiled=True),
    )

    def scan_back(query_acc, blocks):
        query_term, key_term, value_term = back_terms(blocks)
        return (query_acc + query_term, (key_term, value_term))

    query_grad, key_value = lax.scan(
        scan_back,
        jnp.zeros(weighted.shape, jnp.float32),
        tuple(
            (
                member.reshape((block_count, stride * row_count) + member.shape[1:])
                for member in gathered
            )
        ),
    )
    key_parts = key_value[0].reshape(whole_shape)
    value_parts = key_value[1].reshape(whole_shape)
    key_grad, value_grad = (
        lax.psum_scatter(
            key_parts.astype(jnp.bfloat16), "ctx", scatter_dimension=0, tiled=True
        ).astype(jnp.float32),
        lax.psum_scatter(
            value_parts.astype(jnp.bfloat16), "ctx", scatter_dimension=0, tiled=True
        ).astype(jnp.float32),
    )
    d_query = join_heads(query_grad).astype(jnp.bfloat16)
    return (
        step_loss,
        d_query,
        key_grad.astype(jnp.bfloat16),
        value_grad.astype(jnp.bfloat16),
        reward_grad.reshape(head_count, head_size),
    )


def solution(mesh):
    in_specs = (
        P(("dp", "ctx"), "head", None),
        P(("dp", "ctx"), "head", None),
        P(("dp", "ctx"), "head", None),
        P(("dp", "ctx")),
        P("dp"),
        P("dp"),
        P(("dp", "ctx"), "head", None),
        P("head", None),
    )
    out_specs = (
        P("dp"),
        P(("dp", "ctx"), "head", None),
        P(("dp", "ctx"), "head", None),
        P(("dp", "ctx"), "head", None),
        P(("dp", "head"), None),
    )
    return jax.shard_map(local, mesh=mesh, in_specs=in_specs, out_specs=out_specs, check_vma=False)
```

profile of v0, /device:TPU:2, one launch (start us, length us, event | category | flops | bytes accessed | tf_op | source)
XLA Modules:
  0.0 999.6 jit_solution(6048230810022266328)
XLA Ops:
  9.5 41.4 %all-gather = s32[32,1,128]{2,1,0:T(1,128)S(1)} all-gather(s32[1,1,128]{2,1,0:T(1,128)} %bitcast.188), channel_id=1, replica_groups=mesh['ctx'=32,'head'=4,'dp'=2] {'ctx'}, dimensions={0}, use_global_device_ids=true | all-gather | bytes 16896 | tf_op jit(solution)/shard_map/all_gather | solution.py:97
  57.6 31.1 %all-gather.4.cloned.1.call-done = bf16[4096,1,128]{2,0,1:T(8,128)(2,1)} async-done(((bf16[128,1,128]{2,0,1:T(8,128)(2,1)}), bf16[4096,1,128]{2,0,1:T(8,128)(2,1)}) %all-gather.4.cloned.1.call-update) | async-done | bytes 1048592 | tf_op jit(solution)/shard_map/all_gather | solution.py:95
  88.8 4.4 fusion.20
  93.2 5.7 copy-done
  98.9 5.5 fusion.21
  104.5 57.0 %all-gather.6.cloned.1.call-done = bf16[4096,1,128]{0,2,1:T(8,128)(2,1)} async-done(((bf16[128,1,128]{0,2,1:T(8,128)(2,1)}), bf16[4096,1,128]{0,2,1:T(8,128)(2,1)}) %all-gather.6.cloned.1.call-update) | async-done | bytes 1048592 | tf_op jit(solution)/shard_map/all_gather | solution.py:96
  161.5 10.5 %fusion.39 = (f32[128]{0:T(128)S(1)}, bf16[8,128,128]{1,2,0:T(8,128)(2,1)S(1)}) fusion(f32[8,128]{1,0:T(8,128)S(1)} %convert_element_type.88, f32[8,128]{1,0:T(8,128)S(1)} %fusion.21, bf16[4096,1,128]{0,2,1:T(8,128)(2,1)} %all-gather.6.cloned.1.call-done, f32[8,128,4096]{2,1,0:T(8,128)} %copy-done, f32[8,128]{1,0:T(8,128)S(1)} %broadcast_maximum_fusion, ...), kind=kOutput, calls=%fused_computation.43 | convolution fusion | flops 1095368576 | bytes 18625024 | tf_op jit(solution)/shard_map/gjln,ngd->gjld/dot_general | solution.py:39
  172.2 313.2 %psum.14 = f32[64]{0:T(128)S(1)} all-reduce(f32[64]{0:T(128)S(1)} %convolution_bitcast_fusion.3), channel_id=1, replica_groups=mesh['ctx'=32,'head'=4,'dp'=2] {'ctx','head'}, use_global_device_ids=true, to_apply=%region_4.5 | all-reduce | flops 64 | bytes 512 | tf_op jit(solution)/shard_map/psum | solution.py:112
  487.3 69.0 %while.15 = (s32[]{:T(128)}, f32[1,8,128,128]{3,2,1,0:T(8,128)}, bf16[8,512,1,128]{3,1,2,0:T(8,128)(2,1)}, bf16[8,512,1,128]{3,1,2,0:T(8,128)(2,1)}, s32[8,512]{...) while((s32[]{:T(128)}, f32[1,8,128,128]{3,2,1,0:T(8,128)}, ...), condition=%wide.region_7.8_spmd.clone, body=%wide.region_6.7_spmd.clone.sunk | while | flops 675610624 | bytes 12600467 | solution.py:141
  492.5 2.2 fusion.98
  498.9 2.0 fusion.99
  500.9 2.4 fusion.98
  509.6 2.4 fusion.98
  516.2 2.0 fusion.99
  518.2 2.4 fusion.98
  526.9 2.4 fusion.98
  535.5 2.4 fusion.98
  544.2 2.4 fusion.98
  550.8 2.0 fusion.99
  552.8 2.4 fusion.98
  556.9 2.1 copy.52
  560.2 83.2 %psum.15 = f32[8,128]{1,0:T(8,128)} all-reduce(f32[8,128]{1,0:T(8,128)S(1)} %bitcast.189), channel_id=1, replica_groups=mesh['ctx'=32,'head'=4,'dp'=2] {'ctx'}, use_global_device_ids=true, to_apply=%region_10.11 | all-reduce | flops 1024 | bytes 8192 | tf_op jit(solution)/shard_map/psum | solution.py:118
  644.0 132.3 %reduce-scatter.3.cloned.1.call-done = bf16[128,1,128]{2,0,1:T(8,128)(2,1)} async-done(((bf16[4096,1,128]{2,0,1:T(8,128)(2,1)}), bf16[128,1,128]{2,0,1:T(8,128)(2,1)}) %reduce-scatter.3.cloned.1.call-update) | async-done | bytes 32784 | tf_op jit(solution)/shard_map/reduce_scatter | solution.py:154
  776.3 216.9 %reduce-scatter.5.cloned.1.call-done = bf16[128,1,128]{2,0,1:T(8,128)(2,1)} async-done(((bf16[4096,1,128]{2,0,1:T(8,128)(2,1)}), bf16[128,1,128]{2,0,1:T(8,128)(2,1)}) %reduce-scatter.5.cloned.1.call-update) | async-done | bytes 32784 | tf_op jit(solution)/shard_map/reduce_scatter | solution.py:157
  (85 shorter events, 57.2 us)
Async XLA Ops:
  7.2 81.6 %all-gather.4.cloned.1.call-start = ((), (), s32[]{:S(2)}) async-start(), calls=%async_computation.2 | async-start | bytes 1081344 | tf_op jit(solution)/shard_map/all_gather | solution.py:95
  7.9 153.6 %all-gather.6.cloned.1.call-start = ((), (), s32[]{:S(2)}) async-start(), calls=%async_computation.3 | async-start | bytes 1081344 | tf_op jit(solution)/shard_map/all_gather | solution.py:96
  9.4 766.8 %reduce-scatter.3.cloned.1.call-start = ((), (), s32[]{:S(2)}) async-start(), calls=%async_computation.4 | async-start | bytes 1081344 | tf_op jit(solution)/shard_map/reduce_scatter | solution.py:154
  93.2 5.7 copy-start
  104.5 67.6 %copy-start.3 = (s32[128]{0:T(128)S(1)}, s32[128]{0:T(128)}, u32[]{:S(2)}) copy-start(s32[128]{0:T(128)} %param.13) | copy-start | bytes 1540
  104.5 380.9 %copy-start.4 = (s32[64]{0:T(128)S(1)}, s32[64]{0:T(128)}, u32[]{:S(2)}) copy-start(s32[64]{0:T(128)} %param.15) | copy-start | bytes 772
  161.5 324.5 %copy-start.1 = (bf16[4096,1,128]{0,2,1:T(8,128)(2,1)S(1)}, bf16[4096,1,128]{0,2,1:T(8,128)(2,1)}, u32[]{:S(2)}) copy-start(bf16[4096,1,128]{0,2,1:T(8,128)(2,1)} %all-gather.6.cloned.1.call-done) | copy-start | bytes 3145732
  172.0 315.3 %copy-start.2 = (bf16[8,128,128]{1,2,0:T(8,128)(2,1)}, bf16[8,128,128]{1,2,0:T(8,128)(2,1)S(1)}, u32[]{:S(2)}) copy-start(bf16[8,128,128]{1,2,0:T(8,128)(2,1)S(1)} %get-tuple-element.176) | copy-start | bytes 786436
  556.3 436.8 %reduce-scatter.5.cloned.1.call-start = ((), (), s32[]{:S(2)}) async-start(), calls=%async_computation.5 | async-start | bytes 1081344 | tf_op jit(solution)/shard_map/reduce_scatter | solution.py:157
Sparse Core Ops, SparseCore 0:
  10.6 78.1 all-gather.3
  91.8 69.6 all-gather.5
  556.5 219.7 reduce-scatter.2
  780.5 212.5 reduce-scatter.4
where the time goes:
time: 1000 us
  waiting for transfers between devices  439 us (44%)
  blocking collectives  438 us (44%)
  matrix products  84.2 us (8%)
  local copies, waits for them, and re-layouts  14.9 us (1%)
  between operations  13.9 us (1%)
    psum x1, blocking collectives, local(): lax.psum(jnp.dot(owned, row_score, precision=lax.Precision.HIGHEST), ('ct...  313 us
    reduce_scatter x1, waiting for transfers between devices, local(): lax.psum_scatter(value_parts.astype(jnp.bfloat16), 'ctx', scatter_dimensi...  217 us
    reduce_scatter x1, waiting for transfers between devices, local(): lax.psum_scatter(key_parts.astype(jnp.bfloat16), 'ctx', scatter_dimension...  132 us
    psum x1, blocking collectives, local(): reward_grad = lax.psum(local_grad, 'ctx')  83.2 us
    all_gather x1, waiting for transfers between devices, local(): lax.all_gather(value_rows, 'ctx', axis=0, tiled=True)  57 us
    all_gather x1, blocking collectives, local(): lax.all_gather(token_pos, 'ctx', axis=0, tiled=True)  41.4 us
    all_gather x1, waiting for transfers between devices, local(): lax.all_gather(key_rows, 'ctx', axis=0, tiled=True)  31.1 us
  transfers between devices with their start and end apart: 4, of which 4 were waited for; matrix products, arithmetic and copies ran while one was open for 2% of the time, Pallas kernels for 0%

commit v1 on v0

v1 whole, which is shorter than its diff:
```python
import functools
import math

import jax
import jax.numpy as jnp
from jax import lax
from jax.experimental import pallas as pl
from jax.experimental.pallas import tpu as pltpu
from jax.sharding import PartitionSpec as P

MESH = pl.DeviceIdType.MESH
F32, BF16 = jnp.float32, jnp.bfloat16
NX = 4
HD = 128
LD = 128
GROUP = 8
HALF = 64
ROWS = LD * GROUP
RHALF = HALF * GROUP
META = 16
STEPS = 64
ROLLOUTS = 8
SCALE = 1.0 / math.sqrt(HD)
LOG2E = math.log2(math.e)
C2 = SCALE * LOG2E
NEG = -1e30
A, B = slice(0, RHALF), slice(RHALF, ROWS)
EXACT = lax.Precision.HIGHEST


def nn(a, b, precision=None):
    return lax.dot_general(a, b, (((1,), (0,)), ((), ())), precision=precision, preferred_element_type=F32)


def nt(a, b, precision=None):
    return lax.dot_general(a, b, (((1,), (1,)), ((), ())), precision=precision, preferred_element_type=F32)


def tn(a, b):
    return lax.dot_general(a, b, (((0,), (0,)), ((), ())), preferred_element_type=F32)


def col_max(s):
    return jnp.max(s, axis=0, keepdims=True)


def col_sum(s):
    return jnp.sum(s, axis=0, keepdims=True)


def kernel(
    nz, nh,
    pos_ref, step_ref, label_ref, rw_ref, q_ref, g_ref, k_ref, v_ref,
    loss_ref, dq_ref, dk_ref, dv_ref, dr_ref,
    k_all, v_all, qn, qt, gn, gt, rwt, top_s, tot_s, out_s, dq_s, lse_s, delta_s,
    hx, tx, tz, tmine,
    s_kr, r_kr, s_kl, r_kl, p_k, s_kx, r_kx,
    p_v, f_v, c_v, r_v1, r_v2, s_vr, r_vr, s_vl, r_vl, dk_d, dv_d,
    send_sem, k_sem, v_sem, h_sem, tx_sem, tz_sem,
    kr_sem, kl_sem, kx_sem, fv_sem, v1_sem, v2_sem, vr_sem, vl_sem,
):
    far = nz // 2
    me = lax.axis_index("ctx")
    hd = lax.axis_index("head")
    z, x = me // NX, me % NX

    def zi(dz):
        return lax.rem(z + (dz + nz), nz)

    def xi(dx):
        return lax.rem(x + (dx + NX), NX)

    def xdev(dx):
        return {"ctx": z * NX + xi(dx)}

    def zdev(dz):
        return {"ctx": zi(dz) * NX + x}

    def hdev(dh):
        return {"head": lax.rem(hd + dh, nh)}

    def slot(dz, dx):
        return zi(dz) * NX + xi(dx)

    sends = []

    def send(src, dst, recv, dev):
        copy = pltpu.make_async_remote_copy(
            src_ref=src, dst_ref=dst, send_sem=send_sem.at[len(sends)], recv_sem=recv,
            device_id=dev, device_id_type=MESH,
        )
        copy.start()
        sends.append(copy)

    def arrived(dst, recv):
        pltpu.make_async_remote_copy(
            src_ref=dst, dst_ref=dst, send_sem=send_sem.at[0], recv_sem=recv,
            device_id=xdev(1), device_id_type=MESH,
        ).wait_recv()

    def send_k(at, dev):
        send(k_all.at[at], k_all.at[at], k_sem.at[at], dev)

    def send_v(at, dev):
        send(v_all.at[at], v_all.at[at], v_sem.at[at], dev)

    pos = pos_ref[...].astype(F32)
    first, second = pos[:, 0:1], pos[:, HALF:HALF + 1]
    span_f = jnp.minimum(first, second) * (1.0 / HALF)
    later_first = jnp.where(first > second, 1.0, 0.0)

    def ordered(value):
        n = value.shape[0] // 2
        one, two = value[:n].astype(F32), value[n:].astype(F32)
        swap = jnp.broadcast_to(later_first, one.shape) > 0.5
        return jnp.where(swap, two, one).astype(BF16), jnp.where(swap, one, two).astype(BF16)

    k_all[me, 0:HALF], k_all[me, HALF:LD] = ordered(k_ref[...])
    k_all[me, LD:] = jnp.broadcast_to(span_f, (META, HD)).astype(BF16)
    v_all[me, 0:HALF], v_all[me, HALF:LD] = ordered(v_ref[...])

    barrier = pltpu.get_barrier_semaphore()
    peers = [xdev(d) for d in range(1, NX)] + [zdev(d) for d in range(1, nz)] + [hdev(d) for d in range(1, nh)]
    for dev in peers:
        pl.semaphore_signal(barrier, inc=1, device_id=dev, device_id_type=MESH)
    pl.semaphore_wait(barrier, len(peers))

    for dx in (1, 3, 2):
        send_k(me, xdev(dx))
    send_k(me, zdev(1))
    send_k(me, zdev(-1))
    send_v(me, zdev(1))
    send_v(me, zdev(-1))
    send_v(me, xdev(1))
    send_v(me, xdev(-1))

    qn[A], qn[B] = ordered(q_ref[...])
    gn[A], gn[B] = ordered(g_ref[...])
    qt[...] = qn[...].T
    gt[...] = gn[...].T
    rw = rw_ref[...].astype(F32)
    rwt[...] = jnp.broadcast_to(rw[None], (LD, GROUP, HD)).reshape(ROWS, HD).T
    key_tok = lax.broadcasted_iota(jnp.int32, (HALF, RHALF), 0)
    row_tok = lax.broadcasted_iota(jnp.int32, (HALF, RHALF), 1) // GROUP
    tri = jnp.where(key_tok <= row_tok, 0.0, NEG)
    for rows, keys in ((A, slice(0, HALF)), (B, slice(HALF, LD))):
        s = nn(k_all[me, keys], qt[:, rows]) + tri
        top = col_max(s)
        p = jnp.exp2((s - top) * C2)
        top_s[:, rows] = top
        tot_s[:, rows] = col_sum(p)
        out_s[:, rows] = tn(v_all[me, keys], p.astype(BF16))

    def keys_of(ref, zz, half):
        return ref[pl.ds(zz * NX, NX), half * HALF:(half + 1) * HALF, :].reshape(NX * HALF, HD)

    def bias_of(zz, earlier):
        runs = k_all[pl.ds(zz * NX, NX), LD:, :].astype(F32)[:, 0:8, :]
        seen = (runs < span_f) if earlier else (runs > span_f)
        bias = jnp.where(seen, 0.0, NEG)
        bias = jnp.concatenate([bias] * (RHALF // HD), axis=-1)
        return jnp.broadcast_to(bias[:, None], (NX, HALF // 8, 8, RHALF)).reshape(NX * HALF, RHALF)

    def attend(dz):
        zz = zi(dz)
        kl, ku, vl, vu = (keys_of(r, zz, h) for r in (k_all, v_all) for h in (0, 1))
        s = nn(kl, qt[:, A]) + bias_of(zz, True)
        old = top_s[:, A]
        top = jnp.maximum(old, col_max(s))
        p = jnp.exp2((s - top) * C2)
        keep = jnp.exp2((old - top) * C2)
        top_s[:, A] = top
        tot_s[:, A] = tot_s[:, A] * keep + col_sum(p)
        out_s[:, A] = out_s[:, A] * keep + tn(vl, p.astype(BF16))
        s1 = nn(kl, qt[:, B])
        s2 = nn(ku, qt[:, B]) + bias_of(zz, False)
        old = top_s[:, B]
        top = jnp.maximum(old, jnp.maximum(col_max(s1), col_max(s2)))
        p1 = jnp.exp2((s1 - top) * C2)
        p2 = jnp.exp2((s2 - top) * C2)
        keep = jnp.exp2((old - top) * C2)
        top_s[:, B] = top
        tot_s[:, B] = tot_s[:, B] * keep + (col_sum(p1) + col_sum(p2))
        out_s[:, B] = out_s[:, B] * keep + (tn(vl, p1.astype(BF16)) + tn(vu, p2.astype(BF16)))

    def ring(s):
        return [0] if s == 0 else ([far] if s == far else [-s, s])

    def take_k(s):
        if s == 0:
            for dx in (1, 3, 2):
                at = slot(0, dx)
                arrived(k_all.at[at], k_sem.at[at])
                send_k(at, zdev(1))
                send_k(at, zdev(-1))
            return
        for xx in range(NX):
            for dz in ring(s):
                at = zi(dz) * NX + xx
                arrived(k_all.at[at], k_sem.at[at])
                if s + 1 < far or (s + 1 == far and (xx < NX // 2) == (dz < 0)):
                    send_k(at, zdev(1 if dz < 0 else -1))

    def take_vz(s):
        for dz in ring(s):
            at = slot(dz, 0)
            arrived(v_all.at[at], v_sem.at[at])
            if s + 1 < far or (s + 1 == far and dz < 0):
                send_v(at, zdev(1 if dz < 0 else -1))
            send_v(at, xdev(1))
            send_v(at, xdev(-1))

    def take_vx(s):
        for dz in ring(s):
            for dx in (-1, 1):
                at = slot(dz, dx)
                arrived(v_all.at[at], v_sem.at[at])
                if (dz % 2 == 0) == (dx < 0):
                    send_v(at, xdev(-dx))

    def take_v2(dz):
        at = slot(dz, 2)
        arrived(v_all.at[at], v_sem.at[at])

    for s in range(far + 1):
        take_k(s)
        if s + 1 <= far:
            take_vz(s + 1)
        take_vx(s)
        if s:
            for dz in ring(s - 1):
                take_v2(dz)
                attend(dz)
    take_v2(far)
    attend(far)

    total = tot_s[...]
    att = (out_s[...] * (1.0 / total)).astype(BF16).astype(F32)
    out_s[...] = att
    lse_s[...] = top_s[...] * C2 + jnp.log2(total)
    row_of = lax.broadcasted_iota(jnp.int32, (ROWS, LD), 0)
    tok_of = lax.broadcasted_iota(jnp.int32, (ROWS, LD), 1)
    gather_tok = jnp.where(row_of // GROUP == tok_of, 1.0, 0.0)
    score = nn(jnp.broadcast_to(col_sum(att * rwt[...]), (8, ROWS)), gather_tok, EXACT)
    hx[hd] = score
    for dh in range(1, nh):
        send(hx.at[hd], hx.at[hd], h_sem.at[hd], hdev(dh))
    s_of = lax.broadcasted_iota(jnp.int32, (STEPS, STEPS), 0)
    t_of = lax.broadcasted_iota(jnp.int32, (STEPS, STEPS), 1)
    lens = jnp.broadcast_to(step_ref[...].astype(F32), (STEPS, STEPS))
    ends = jnp.sum(jnp.where(t_of <= s_of, lens, 0.0), axis=1, keepdims=True) - 1.0
    lane = lax.broadcasted_iota(jnp.int32, (1, LD), 1)
    last_span = nz * NX * 2 - 1
    run = jnp.where(lane < HALF, span_f, last_span - span_f)
    tok_pos = run * HALF + (lane % HALF).astype(F32)
    owned = jnp.where(ends == tok_pos, 1.0, 0.0)
    target = label_ref[...].astype(F32) / ROLLOUTS
    tok_target = nn(jnp.broadcast_to(target, (8, STEPS)), owned, EXACT)
    is_end = col_sum(owned)
    for dh in range(1, nh):
        at = lax.rem(hd + dh, nh)
        arrived(hx.at[at], h_sem.at[at])
    logit = hx[0]
    for h in range(1, nh):
        logit = logit + hx[h]
    misfit = (jax.nn.sigmoid(logit) - tok_target) * is_end
    row_of = lax.broadcasted_iota(jnp.int32, (LD, ROWS), 1)
    tok_of = lax.broadcasted_iota(jnp.int32, (LD, ROWS), 0)
    spread = jnp.where(row_of // GROUP == tok_of, 1.0, 0.0)
    weight = nn(misfit, spread, EXACT)[0:1]
    grad = (gt[...].astype(F32) + weight * rwt[...]).astype(BF16)
    gt[...] = grad
    gn[...] = grad.T
    delta_s[...] = col_sum(grad.astype(F32) * att)
    head_of = lax.broadcasted_iota(jnp.int32, (GROUP, ROWS), 0)
    row_of = lax.broadcasted_iota(jnp.int32, (GROUP, ROWS), 1)
    pick = jnp.where(row_of % GROUP == head_of, 1.0, 0.0)
    tmine[0:8] = nt(pick, att * weight, EXACT)
    own_logits = nt(logit, owned, EXACT)
    tmine[8:16] = jnp.concatenate([own_logits, jnp.zeros_like(own_logits)], axis=1)
    tx[x] = tmine[...]
    for dx in (1, 3, 2):
        send(tx.at[x], tx.at[x], tx_sem.at[x], xdev(dx))

    def totals_x():
        for dx in (1, 3, 2):
            at = xi(dx)
            arrived(tx.at[at], tx_sem.at[at])
        tz[z] = tx[0] + tx[1] + tx[2] + tx[3]
        for dz in range(1, nz):
            send(tz.at[z], tz.at[z], tz_sem.at[z], zdev(dz))

    def totals_z():
        for dz in range(1, nz):
            at = zi(dz)
            arrived(tz.at[at], tz_sem.at[at])
        both = tz[0]
        for i in range(1, nz):
            both = both + tz[i]
        dr_ref[...] = both[0:8]
        logits = both[8:9, 0:STEPS]
        soft = jnp.maximum(logits, 0.0) + jnp.log1p(jnp.exp(-jnp.abs(logits)))
        loss_ref[...] = soft - target * logits

    dq_s[...] = jnp.zeros(dq_s.shape, F32)

    def back(k, v, rows, bias):
        s = nn(k, qt[:, rows])
        if bias is not None:
            s = s + bias
        p = jnp.exp2(s * C2 - lse_s[:, rows])
        ds = (p * (nn(v, gt[:, rows]) - delta_s[:, rows])).astype(BF16)
        dq_s[:, rows] += tn(k, ds)
        return nn(ds, qn[rows]), nn(p.astype(BF16), gn[rows])

    def back_group(dz):
        zz = zi(dz)
        kl, ku, vl, vu = (keys_of(r, zz, h) for r in (k_all, v_all) for h in (0, 1))
        k1, v1 = back(kl, vl, A, bias_of(zz, True))
        k2, v2 = back(kl, vl, B, None)
        k3, v3 = back(ku, vu, B, bias_of(zz, False))
        p_k[:, 0:HALF] = ((k1 + k2) * SCALE).reshape(NX, HALF, HD)
        p_k[:, HALF:LD] = (k3 * SCALE).reshape(NX, HALF, HD)
        return (v1 + v2).reshape(NX, HALF, HD), v3.reshape(NX, HALF, HD)

    def wide(ref):
        return ref[...].astype(F32)

    order = [far]
    for s in range(far - 1, 0, -1):
        order += [s, -s]
    order += [0]
    two = NX // 2

    def pass_k(dz):
        if dz == far:
            s_kr[far, 0:two] = p_k[0:two].astype(BF16)
            s_kl[far, two:] = p_k[two:].astype(BF16)
            send(s_kr.at[far, 0:two], r_kr.at[far, 0:two], kr_sem.at[far, 0], zdev(1))
            send(s_kl.at[far, two:], r_kl.at[far, two:], kl_sem.at[far, 1], zdev(-1))
            return
        d = abs(dz)
        s_k, r_k, sem = (s_kr, r_kr, kr_sem) if dz > 0 else (s_kl, r_kl, kl_sem)
        for half in (0, 1):
            part = slice(half * two, (half + 1) * two)
            own = p_k[part]
            if d + 1 < far or (half == 0) == (dz > 0):
                arrived(r_k.at[d + 1, part], sem.at[d + 1, half])
                own = own + wide(r_k.at[d + 1, part])
            s_k[d, part] = own.astype(BF16)
            send(s_k.at[d, part], r_k.at[d, part], sem.at[d, half], zdev(1 if dz > 0 else -1))

    def give_v(i):
        way = 1 if order[i] % 2 == 0 else -1
        send(p_v.at[i, xi(2)], f_v.at[i], fv_sem.at[i], xdev(way))
        send(p_v.at[i, xi(-way)], r_v1.at[i], v1_sem.at[i], xdev(-way))

    def relay_v(i):
        way = 1 if order[i] % 2 == 0 else -1
        arrived(f_v.at[i], fv_sem.at[i])
        c_v[i] = (p_v[i, xi(way)].astype(F32) + wide(f_v.at[i])).astype(BF16)
        send(c_v.at[i], r_v2.at[i], v2_sem.at[i], xdev(way))

    def pass_v(i):
        dz = order[i]
        arrived(r_v1.at[i], v1_sem.at[i])
        arrived(r_v2.at[i], v2_sem.at[i])
        total = p_v[i, x].astype(F32) + wide(r_v1.at[i]) + wide(r_v2.at[i])
        if dz > 0:
            if dz < far:
                arrived(r_vr.at[dz + 1], vr_sem.at[dz + 1])
                total = total + wide(r_vr.at[dz + 1])
            s_vr[dz] = total.astype(BF16)
            send(s_vr.at[dz], r_vr.at[dz], vr_sem.at[dz], zdev(1))
        elif dz < 0:
            d = -dz
            if d + 1 < far:
                arrived(r_vl.at[d + 1], vl_sem.at[d + 1])
                total = total + wide(r_vl.at[d + 1])
            s_vl[d] = total.astype(BF16)
            send(s_vl.at[d], r_vl.at[d], vl_sem.at[d], zdev(-1))
        else:
            arrived(r_vr.at[1], vr_sem.at[1])
            arrived(r_vl.at[1], vl_sem.at[1])
            dv_d[...] += total + wide(r_vr.at[1]) + wide(r_vl.at[1])

    for i, dz in enumerate(order):
        v_lo, v_hi = back_group(dz)
        p_v[i, :, 0:HALF] = v_lo.astype(BF16)
        p_v[i, :, HALF:LD] = v_hi.astype(BF16)
        give_v(i)
        if dz:
            pass_k(dz)
        if i >= 1:
            relay_v(i - 1)
        if i >= 2:
            pass_v(i - 2)
        if i == 1:
            totals_x()
    last = len(order) - 1
    relay_v(last)
    for half in (0, 1):
        part = slice(half * two, (half + 1) * two)
        arrived(r_kr.at[1, part], kr_sem.at[1, half])
        arrived(r_kl.at[1, part], kl_sem.at[1, half])
    s_kx[...] = (p_k[...] + wide(r_kr.at[1]) + wide(r_kl.at[1])).astype(BF16)
    for dx in (1, 3, 2):
        send(s_kx.at[xi(dx)], r_kx.at[dx], kx_sem.at[dx], xdev(dx))
    pass_v(last - 1)
    for rows, keys in ((A, slice(0, HALF)), (B, slice(HALF, LD))):
        dk_own, dv_own = back(k_all[me, keys], v_all[me, keys], rows, tri)
        dk_d[keys], dv_d[keys] = dk_own * SCALE, dv_own
    dq_ref[A], dq_ref[B] = ordered((dq_s[...] * SCALE).T)
    pass_v(last)
    dv_ref[0:HALF], dv_ref[HALF:LD] = ordered(dv_d[...])
    totals_z()
    for dx in (1, 3, 2):
        arrived(r_kx.at[dx], kx_sem.at[dx])
    dk_d[...] += s_kx[x].astype(F32) + wide(r_kx.at[1]) + wide(r_kx.at[2]) + wide(r_kx.at[3])
    dk_ref[0:HALF], dk_ref[HALF:LD] = ordered(dk_d[...])
    for copy in sends:
        copy.wait_send()


def local(nz, nh, queries, key_rows, value_rows, token_pos, step_len, label_count, out_grad, reward_weight):
    far, n = nz // 2, nz * NX
    vmem = pl.BlockSpec(memory_space=pltpu.VMEM)
    block = (LD, HD)
    scratch = [
        ((n, LD + META, HD), BF16), ((n,) + block, BF16),
        ((ROWS, HD), BF16), ((HD, ROWS), BF16), ((ROWS, HD), BF16), ((HD, ROWS), BF16), ((HD, ROWS), F32),
        ((1, ROWS), F32), ((1, ROWS), F32), ((HD, ROWS), F32), ((HD, ROWS), F32), ((1, ROWS), F32), ((1, ROWS), F32),
        ((nh, 8, HD), F32), ((NX, 16, HD), F32), ((nz, 16, HD), F32), ((16, HD), F32),
    ]
    chain = ((far + 1, NX) + block, BF16)
    scratch += [chain] * 4 + [((NX,) + block, F32), ((NX,) + block, BF16), ((NX,) + block, BF16)]
    steps = ((nz,) + block, BF16)
    scratch += [((nz, NX) + block, BF16), steps, steps, steps, steps] + [((far + 1,) + block, BF16)] * 4
    scratch += [(block, F32), (block, F32)]
    dma = lambda *shape: pltpu.SemaphoreType.DMA(shape)
    sems = [
        dma(256), dma(n), dma(n), dma(nh), dma(NX), dma(nz),
        dma(far + 1, 2), dma(far + 1, 2), dma(NX), dma(nz), dma(nz), dma(nz), dma(far + 1), dma(far + 1),
    ]
    loss, dq, dk, dv, dr = pl.pallas_call(
        functools.partial(kernel, nz, nh),
        out_shape=[
            jax.ShapeDtypeStruct((1, STEPS), F32),
            jax.ShapeDtypeStruct((ROWS, HD), BF16),
            jax.ShapeDtypeStruct(block, BF16),
            jax.ShapeDtypeStruct(block, BF16),
            jax.ShapeDtypeStruct((GROUP, HD), F32),
        ],
        in_specs=[vmem] * 8,
        out_specs=[vmem] * 5,
        scratch_shapes=[pltpu.VMEM(s, t) for s, t in scratch] + sems,
        compiler_params=pltpu.CompilerParams(
            collective_id=0, has_side_effects=True, vmem_limit_bytes=48 * 2**20
        ),
    )(
        token_pos.reshape(1, LD),
        step_len.reshape(1, STEPS),
        label_count.reshape(1, STEPS),
        reward_weight,
        queries.reshape(ROWS, HD),
        out_grad.reshape(ROWS, HD),
        key_rows.reshape(block),
        value_rows.reshape(block),
    )
    return (
        loss.reshape(STEPS),
        dq.reshape(queries.shape),
        dk.reshape(key_rows.shape),
        dv.reshape(value_rows.shape),
        dr,
    )


def solution(mesh):
    rows = P(("dp", "ctx"), "head", None)
    return jax.shard_map(
        functools.partial(local, mesh.shape["ctx"] // NX, mesh.shape["head"]),
        mesh=mesh,
        in_specs=(rows, rows, rows, P(("dp", "ctx")), P("dp"), P("dp"), rows, P("head", None)),
        out_specs=(P("dp"), rows, rows, rows, P(("dp", "head"), None)),
        check_vma=False,
    )
```

time: 1000 us -> 79.5 us (0.08)
  waiting for transfers between devices: 439 us -> 0 us
  blocking collectives: 438 us -> 0 us
  matrix products: 84.2 us -> 0 us
  Pallas kernels: 0 us -> 70.9 us
  between operations: 13.9 us -> 0.68 us
    psum x2 -> x0, blocking collectives: 396 us -> none  [the longest x1 313 us: local(): lax.psum(jnp.dot(owned, row_score, precision=lax.Precision.HIGHEST), ('ct...]
    reduce_scatter x2 -> x0, waiting for transfers between devices: 349 us -> none  [the longest x1 217 us: local(): lax.psum_scatter(value_parts.astype(jnp.bfloat16), 'ctx', scatter_dimensi...]
    all_gather x2 -> x0, waiting for transfers between devices: 88.1 us -> none  [the longest x1 57 us: local(): lax.all_gather(value_rows, 'ctx', axis=0, tiled=True)]
    dot_general x44 -> x0, matrix products: 83 us -> none  [the longest x8 18.9 us: back_block(): jnp.einsum('gjln,ngd->gjld', grad_score, key_block, preferred_element_typ...]
    pallas_call x0 -> x1, Pallas kernels: none -> 70.9 us  [local(): pl.pallas_call(functools.partial(kernel, nz, nh), out_shape=[jax.ShapeDty...]
    all_gather x1 -> x0, blocking collectives: 41.4 us -> none  [local(): lax.all_gather(token_pos, 'ctx', axis=0, tiled=True)]
  transfers between devices with their start and end apart: 4 -> 0, of which waited for: 4 -> 0; matrix products, arithmetic and copies ran while one was open for 2% -> 0% of each run, Pallas kernels for 0% -> 0%
where the time goes in v1:
time: 79.5 us; the launch traced here: 78.7 us
  Pallas kernels  70.9 us (89%)
  local copies, waits for them, and re-layouts  7.12 us (9%)
    pallas_call x1, Pallas kernels, local(): pl.pallas_call(functools.partial(kernel, nz, nh), out_shape=[jax.ShapeDty...  70.9 us
    unnamed x21, local copies, waits for them, and re-layouts  7.12 us

profile of v1, /device:TPU:2, one launch (start us, length us, event | category | flops | bytes accessed | tf_op | source)
XLA Modules:
  0.0 78.7 jit_solution(6088837941678232612)
XLA Ops:
  0.6 0.0 copy-start.4
  0.6 0.0 copy-start.5
  0.7 0.0 copy-start.6
  0.7 0.0 copy-start.7
  0.7 0.6 copy-done.4
  1.3 0.0 copy-done.5
  1.3 0.0 copy-done.6
  1.3 0.0 copy-done.7
  1.3 0.0 copy-start
  1.3 0.9 %copy-done = bf16[128,8,128]{2,1,0:T(8,128)(2,1)S(1)} copy-done((bf16[128,8,128]{2,1,0:T(8,128)(2,1)S(1)}, bf16[128,8,128]{2,1,0:T(8,128)(2,1)}, u32[]{:S(2)}) %copy-start) | copy-done | bytes 262168
  2.3 0.0 copy-start.1
  2.3 0.9 %copy-done.1 = bf16[128,8,128]{2,1,0:T(8,128)(2,1)S(1)} copy-done((bf16[128,8,128]{2,1,0:T(8,128)(2,1)S(1)}, bf16[128,8,128]{2,1,0:T(8,128)(2,1)}, u32[]{:S(2)}) %copy-start.1) | copy-done | bytes 262168
  3.2 0.0 copy-start.2
  3.2 0.8 copy-done.2
  4.0 0.0 copy-start.3
  4.0 0.8 copy-done.3
  4.8 70.9 %shard_map.119 = (f32[1,64]{1,0:T(1,128)S(1)}, bf16[1024,128]{1,0:T(8,128)(2,1)S(1)}, bf16[128,128]{1,0:T(8,128)(2,1)S(1)}, bf16[128,128]{1,0:T(8,128)(2,1)S(1)}, f32[8,128]{1,0:T(8,128)S(1)}) custom-call(s32[1,128]{1,0:T(1,128)S(1)} %bitcast.18, s32[1,64]{1,0:T(1,128)S(1)} %bitcast.19, s32[1,64]{1,0:T(1,128)S(1)} %bitcast.20, bf16[8,128]{1,0:T(8,128)(2,1)S(1)} %copy-done.4, ...), custom_call_target="tpu_custom_call" | custom-call | tf_op jit(solution)/shard_map/pallas_call | solution.py:445
  75.7 0.5 copy.18
  76.2 0.7 copy.19
  76.9 0.6 copy.20
  77.5 0.6 copy.21
  78.1 0.6 copy.22
Async XLA Ops:
  0.6 0.7 copy-start.4
  0.6 0.7 copy-start.5
  0.7 0.7 copy-start.6
  0.7 0.7 copy-start.7
  1.3 0.9 %copy-start = (bf16[128,8,128]{2,1,0:T(8,128)(2,1)S(1)}, bf16[128,8,128]{2,1,0:T(8,128)(2,1)}, u32[]{:S(2)}) copy-start(bf16[128,8,128]{2,1,0:T(8,128)(2,1)} %param.8) | copy-start | bytes 786436
  2.3 0.9 %copy-start.1 = (bf16[128,8,128]{2,1,0:T(8,128)(2,1)S(1)}, bf16[128,8,128]{2,1,0:T(8,128)(2,1)}, u32[]{:S(2)}) copy-start(bf16[128,8,128]{2,1,0:T(8,128)(2,1)} %param.14) | copy-start | bytes 786436
  3.2 0.8 copy-start.2
  4.0 0.8 copy-start.3

commit v2 on v1

v2 whole, which is shorter than its diff:
```python
import functools
import math

import jax
import jax.numpy as jnp
from jax import lax
from jax.experimental import pallas as pl
from jax.experimental.pallas import tpu as pltpu
from jax.sharding import PartitionSpec as P

MESH = pl.DeviceIdType.MESH
F32, BF16 = jnp.float32, jnp.bfloat16
NX = 4
HD = 128
LD = 128
GROUP = 8
HALF = 64
ROWS = LD * GROUP
RHALF = HALF * GROUP
META = 16
STEPS = 64
ROLLOUTS = 8
SCALE = 1.0 / math.sqrt(HD)
LOG2E = math.log2(math.e)
C2 = SCALE * LOG2E
NEG = -1e30
A, B = slice(0, RHALF), slice(RHALF, ROWS)
VMEM_BYTES = 60 * 2**20
OTHERS = (1, 3, 2)


def nn(a, b):
    return lax.dot_general(a, b, (((1,), (0,)), ((), ())), preferred_element_type=F32)


def nt(a, b):
    return lax.dot_general(a, b, (((1,), (1,)), ((), ())), preferred_element_type=F32)


def tn(a, b):
    return lax.dot_general(a, b, (((0,), (0,)), ((), ())), preferred_element_type=F32)


def col_max(s):
    return jnp.max(s, axis=0, keepdims=True)


def col_sum(s):
    return jnp.sum(s, axis=0, keepdims=True)


def kernel(
    nz, nh,
    pos_hbm, step_hbm, label_hbm, rw_hbm, q_hbm, g_hbm, k_hbm, v_hbm,
    loss_hbm, dq_hbm, dk_hbm, dv_hbm, dr_hbm,
    loss_ref, dq_ref, dk_ref, dv_ref, dr_ref, pos_ref, step_ref, label_ref, rw_ref, q_ref, g_ref, k_ref, v_ref,
    k_all, v_all, qn, qt, gn, gt, rwt, top_s, tot_s, out_s, dq_s, lse_s, delta_s,
    to_tok, to_row, owned_s, hx, tx, tz,
    s_kr, r_kr, s_kl, r_kl, p_k, s_kx, r_kx,
    p_v, r_v, s_vr, r_vr, s_vl, r_vl, dk_d, dv_d,
    in_sem, out_sem, send_sem, k_sem, v_sem, h_sem, tx_sem, tz_sem,
    kr_sem, kl_sem, kx_sem, rv_sem, vr_sem, vl_sem,
):
    far = nz // 2
    me = lax.axis_index("ctx")
    hd = lax.axis_index("head")
    z, x = me // NX, me % NX

    def zi(dz):
        return lax.rem(z + (dz + nz), nz)

    def xi(dx):
        return lax.rem(x + (dx + NX), NX)

    def xdev(dx):
        return {"ctx": z * NX + xi(dx)}

    def zdev(dz):
        return {"ctx": zi(dz) * NX + x}

    def hdev(dh):
        return {"head": lax.rem(hd + dh, nh)}

    def slot(dz, dx):
        return zi(dz) * NX + xi(dx)

    sends, stores = [], []

    def store(src, dst):
        copy = pltpu.make_async_copy(src, dst, out_sem.at[len(stores)])
        copy.start()
        stores.append(copy)

    def send(src, dst, recv, dev):
        copy = pltpu.make_async_remote_copy(
            src_ref=src, dst_ref=dst, send_sem=send_sem.at[len(sends)], recv_sem=recv,
            device_id=dev, device_id_type=MESH,
        )
        copy.start()
        sends.append(copy)

    def arrived(dst, recv):
        pltpu.make_async_remote_copy(
            src_ref=dst, dst_ref=dst, send_sem=send_sem.at[0], recv_sem=recv,
            device_id=xdev(1), device_id_type=MESH,
        ).wait_recv()

    def send_k(at, dev):
        send(k_all.at[at], k_all.at[at], k_sem.at[at], dev)

    def send_v(at, dev):
        send(v_all.at[at], v_all.at[at], v_sem.at[at], dev)

    barrier = pltpu.get_barrier_semaphore()
    peers = [xdev(d) for d in range(1, NX)] + [zdev(d) for d in range(1, nz)] + [hdev(d) for d in range(1, nh)]
    for dev in peers:
        pl.semaphore_signal(barrier, inc=1, device_id=dev, device_id_type=MESH)
    pairs = [
        (pos_hbm, pos_ref), (k_hbm, k_ref), (v_hbm, v_ref), (q_hbm, q_ref), (g_hbm, g_ref),
        (rw_hbm, rw_ref), (step_hbm, step_ref), (label_hbm, label_ref),
    ]
    loads = [pltpu.make_async_copy(src, dst, in_sem.at[i]) for i, (src, dst) in enumerate(pairs)]
    for load in loads:
        load.start()

    for load in loads[0:3]:
        load.wait()
    pos = pos_ref[...].astype(F32)
    first, second = pos[:, 0:1], pos[:, HALF:HALF + 1]
    span_f = jnp.minimum(first, second) * (1.0 / HALF)
    later_first = jnp.where(first > second, 1.0, 0.0)

    def ordered(value):
        n = value.shape[0] // 2
        one, two = value[:n].astype(F32), value[n:].astype(F32)
        swap = jnp.broadcast_to(later_first, one.shape) > 0.5
        return jnp.where(swap, two, one).astype(BF16), jnp.where(swap, one, two).astype(BF16)

    k_all[me, 0:HALF], k_all[me, HALF:LD] = ordered(k_ref[...])
    k_all[me, LD:] = jnp.broadcast_to(span_f, (META, HD)).astype(BF16)
    v_all[me, 0:HALF], v_all[me, HALF:LD] = ordered(v_ref[...])

    pl.semaphore_wait(barrier, len(peers))

    for give in (send_k, send_v):
        give(me, zdev(1))
        give(me, zdev(-1))
        for dx in OTHERS:
            give(me, xdev(dx))

    for load in loads[3:]:
        load.wait()
    qn[A], qn[B] = ordered(q_ref[...])
    gn[A], gn[B] = ordered(g_ref[...])
    qt[...] = qn[...].T
    gt[...] = gn[...].T
    key_tok = lax.broadcasted_iota(jnp.int32, (HALF, RHALF), 0)
    row_tok = lax.broadcasted_iota(jnp.int32, (HALF, RHALF), 1) // GROUP
    tri = jnp.where(key_tok <= row_tok, 0.0, NEG)
    for rows, keys in ((A, slice(0, HALF)), (B, slice(HALF, LD))):
        s = nn(k_all[me, keys], qt[:, rows]) + tri
        top = col_max(s)
        p = jnp.exp2((s - top) * C2)
        top_s[:, rows] = top
        tot_s[:, rows] = col_sum(p)
        out_s[:, rows] = tn(v_all[me, keys], p.astype(BF16))

    def keys_of(ref, zz, half):
        return ref[pl.ds(zz * NX, NX), half * HALF:(half + 1) * HALF, :].reshape(NX * HALF, HD)

    def bias_of(zz, earlier):
        runs = k_all[pl.ds(zz * NX, NX), LD:, :].astype(F32)[:, 0:8, :]
        seen = (runs < span_f) if earlier else (runs > span_f)
        bias = jnp.where(seen, 0.0, NEG)
        bias = jnp.concatenate([bias] * (RHALF // HD), axis=-1)
        return jnp.broadcast_to(bias[:, None], (NX, HALF // 8, 8, RHALF)).reshape(NX * HALF, RHALF)

    def attend_a(dz):
        zz = zi(dz)
        kl, vl = keys_of(k_all, zz, 0), keys_of(v_all, zz, 0)
        s = nn(kl, qt[:, A]) + bias_of(zz, True)
        old = top_s[:, A]
        top = jnp.maximum(old, col_max(s))
        p = jnp.exp2((s - top) * C2)
        keep = jnp.exp2((old - top) * C2)
        top_s[:, A] = top
        tot_s[:, A] = tot_s[:, A] * keep + col_sum(p)
        out_s[:, A] = out_s[:, A] * keep + tn(vl, p.astype(BF16))

    def attend_b(dz):
        zz = zi(dz)
        kl, ku, vl, vu = (keys_of(r, zz, h) for r in (k_all, v_all) for h in (0, 1))
        s1 = nn(kl, qt[:, B])
        s2 = nn(ku, qt[:, B]) + bias_of(zz, False)
        old = top_s[:, B]
        top = jnp.maximum(old, jnp.maximum(col_max(s1), col_max(s2)))
        p1 = jnp.exp2((s1 - top) * C2)
        p2 = jnp.exp2((s2 - top) * C2)
        keep = jnp.exp2((old - top) * C2)
        top_s[:, B] = top
        tot_s[:, B] = tot_s[:, B] * keep + (col_sum(p1) + col_sum(p2))
        out_s[:, B] = out_s[:, B] * keep + (tn(vl, p1.astype(BF16)) + tn(vu, p2.astype(BF16)))

    def ring(s):
        return [0] if s == 0 else ([far] if s == far else [-s, s])

    def take_k(dz, dx):
        at = slot(dz, dx)
        arrived(k_all.at[at], k_sem.at[at])
        s = abs(dz)
        if s == 0:
            send_k(at, zdev(1))
            send_k(at, zdev(-1))
        elif s + 1 < far or (s + 1 == far and (dx < NX // 2) == (dz < 0)):
            send_k(at, zdev(1 if dz < 0 else -1))

    def take_vz(s):
        for dz in ring(s):
            at = slot(dz, 0)
            arrived(v_all.at[at], v_sem.at[at])
            if s + 1 < far or (s + 1 == far and dz < 0):
                send_v(at, zdev(1 if dz < 0 else -1))
        for dz in ring(s):
            for dx in OTHERS:
                send_v(slot(dz, 0), xdev(dx))

    def take_vx(dz):
        for dx in OTHERS:
            at = slot(dz, dx)
            arrived(v_all.at[at], v_sem.at[at])

    def prepare():
        rw = rw_ref[...].astype(F32)
        rwt[...] = jnp.broadcast_to(rw[None], (LD, GROUP, HD)).reshape(ROWS, HD).T
        row_of = lax.broadcasted_iota(jnp.int32, (ROWS, LD), 0)
        tok_of = lax.broadcasted_iota(jnp.int32, (ROWS, LD), 1)
        to_tok[...] = jnp.where(row_of // GROUP == tok_of, 1.0, 0.0).astype(BF16)
        row_of = lax.broadcasted_iota(jnp.int32, (LD, ROWS), 1)
        tok_of = lax.broadcasted_iota(jnp.int32, (LD, ROWS), 0)
        to_row[...] = jnp.where(row_of // GROUP == tok_of, 1.0, 0.0).astype(BF16)
        s_of = lax.broadcasted_iota(jnp.int32, (STEPS, STEPS), 0)
        t_of = lax.broadcasted_iota(jnp.int32, (STEPS, STEPS), 1)
        lens = jnp.broadcast_to(step_ref[...].astype(F32), (STEPS, STEPS))
        ends = jnp.sum(jnp.where(t_of <= s_of, lens, 0.0), axis=1, keepdims=True) - 1.0
        lane = lax.broadcasted_iota(jnp.int32, (1, LD), 1)
        run = jnp.where(lane < HALF, span_f, (nz * NX * 2 - 1) - span_f)
        tok_pos = run * HALF + (lane % HALF).astype(F32)
        owned_s[...] = jnp.where(ends == tok_pos, 1.0, 0.0)
        dq_s[...] = jnp.zeros(dq_s.shape, F32)

    for s in range(far + 1):
        pieces = []
        if s == 1:
            take_vx(0)
        if s:
            for dz in ring(s - 1):
                pieces += [(attend_a, dz), (attend_b, dz)]
        for i, dx in enumerate((0,) + OTHERS):
            for dz in ring(s):
                if s or dx:
                    take_k(dz, dx)
            if i == 0 and s + 1 <= far:
                take_vz(s + 1)
            if i < len(pieces):
                piece, dz = pieces[i]
                if piece is attend_a and dz:
                    take_vx(dz)
                piece(dz)
        if s == far:
            prepare()
    take_vx(far)
    attend_a(far)
    attend_b(far)

    total = tot_s[...]
    att = (out_s[...] * (1.0 / total)).astype(BF16).astype(F32)
    out_s[...] = att
    lse_s[...] = top_s[...] * C2 + jnp.log2(total)
    def thirds(value):
        one = value.astype(BF16)
        rest = value - one.astype(F32)
        two = rest.astype(BF16)
        return [one, two, (rest - two.astype(F32)).astype(BF16)]

    def rows_of(value):
        pad = jnp.zeros((META - 3,) + value.shape[1:], F32)
        return jnp.concatenate([t.astype(F32) for t in thirds(value)] + [pad], axis=0).astype(BF16)

    score = col_sum(nn(rows_of(col_sum(att * rwt[...])), to_tok[...]))
    hx[hd] = jnp.broadcast_to(score, (8, LD))
    for dh in range(1, nh):
        send(hx.at[hd], hx.at[hd], h_sem.at[hd], hdev(dh))
    owned = owned_s[...]
    owned_low = owned.astype(BF16)
    target = label_ref[...].astype(F32) / ROLLOUTS
    tok_target = nn(jnp.broadcast_to(target, (META, STEPS)).astype(BF16), owned_low)[0:1]
    is_end = col_sum(owned)
    for dh in range(1, nh):
        at = lax.rem(hd + dh, nh)
        arrived(hx.at[at], h_sem.at[at])
    logit = hx[0]
    for h in range(1, nh):
        logit = logit + hx[h]
    logit = logit[0:1]
    misfit = (jax.nn.sigmoid(logit) - tok_target) * is_end
    weight = col_sum(nn(rows_of(misfit), to_row[...]))
    grad = (gt[...].astype(F32) + weight * rwt[...]).astype(BF16)
    gt[...] = grad
    gn[...] = grad.T
    delta_s[...] = col_sum(grad.astype(F32) * att)

    def totals():
        head_of = lax.broadcasted_iota(jnp.int32, (GROUP, ROWS), 0)
        row_of = lax.broadcasted_iota(jnp.int32, (GROUP, ROWS), 1)
        pick = jnp.where(row_of % GROUP == head_of, jnp.broadcast_to(weight, (GROUP, ROWS)), 0.0)
        att_low = out_s[...].astype(BF16)
        parts = [nt(t, att_low) for t in thirds(pick)]
        tx[x, 0:8] = parts[0] + parts[1] + parts[2]
        own = col_sum(nt(rows_of(logit), owned_low))
        tx[x, 8:16] = jnp.broadcast_to(jnp.concatenate([own, jnp.zeros_like(own)], axis=1), (8, LD))
        for dx in OTHERS:
            send(tx.at[x], tx.at[x], tx_sem.at[x], xdev(dx))

    def totals_x():
        for dx in OTHERS:
            at = xi(dx)
            arrived(tx.at[at], tx_sem.at[at])
        tz[z] = tx[0] + tx[1] + tx[2] + tx[3]
        for dz in range(1, nz):
            send(tz.at[z], tz.at[z], tz_sem.at[z], zdev(dz))

    def totals_z():
        for dz in range(1, nz):
            at = zi(dz)
            arrived(tz.at[at], tz_sem.at[at])
        both = tz[0]
        for i in range(1, nz):
            both = both + tz[i]
        dr_ref[...] = both[0:8]
        logits = both[8:9, 0:STEPS]
        soft = jnp.maximum(logits, 0.0) + jnp.log1p(jnp.exp(-jnp.abs(logits)))
        loss_ref[...] = soft - target * logits
        store(dr_ref, dr_hbm)
        store(loss_ref, loss_hbm)

    def back(k, v, rows, bias):
        s = nn(k, qt[:, rows])
        if bias is not None:
            s = s + bias
        p = jnp.exp2(s * C2 - lse_s[:, rows])
        ds = (p * (nn(v, gt[:, rows]) - delta_s[:, rows])).astype(BF16)
        dq_s[:, rows] += tn(k, ds)
        return nn(ds, qn[rows]), nn(p.astype(BF16), gn[rows])

    def back_group(dz):
        zz = zi(dz)
        kl, ku, vl, vu = (keys_of(r, zz, h) for r in (k_all, v_all) for h in (0, 1))
        k1, v1 = back(kl, vl, A, bias_of(zz, True))
        k2, v2 = back(kl, vl, B, None)
        k3, v3 = back(ku, vu, B, bias_of(zz, False))
        p_k[:, 0:HALF] = ((k1 + k2) * SCALE).reshape(NX, HALF, HD)
        p_k[:, HALF:LD] = (k3 * SCALE).reshape(NX, HALF, HD)
        return (v1 + v2).reshape(NX, HALF, HD), v3.reshape(NX, HALF, HD)

    def wide(ref):
        return ref[...].astype(F32)

    order = [far]
    for s in range(far - 1, 0, -1):
        order += [s, -s]
    order += [0]
    two = NX // 2

    def pass_k(dz):
        d = abs(dz)
        for xx in range(NX):
            for right in (True, False):
                crosses = (xx < two) == right
                if (dz == far and not crosses) or (dz != far and (dz > 0) != right):
                    continue
                s_k, r_k, sem = (s_kr, r_kr, kr_sem) if right else (s_kl, r_kl, kl_sem)
                own = p_k[xx]
                if d + 1 < far or (d + 1 == far and crosses):
                    arrived(r_k.at[d + 1, xx], sem.at[d + 1, xx])
                    own = own + wide(r_k.at[d + 1, xx])
                s_k[d, xx] = own.astype(BF16)
                send(s_k.at[d, xx], r_k.at[d, xx], sem.at[d, xx], zdev(1 if right else -1))

    def give_v(i):
        for dx in OTHERS:
            send(p_v.at[i, xi(dx)], r_v.at[i, dx], rv_sem.at[i, dx], xdev(dx))

    def pass_v(i):
        dz = order[i]
        total = p_v[i, x].astype(F32)
        for dx in OTHERS:
            arrived(r_v.at[i, dx], rv_sem.at[i, dx])
            total = total + wide(r_v.at[i, dx])
        if dz > 0:
            if dz < far:
                arrived(r_vr.at[dz + 1], vr_sem.at[dz + 1])
                total = total + wide(r_vr.at[dz + 1])
            s_vr[dz] = total.astype(BF16)
            send(s_vr.at[dz], r_vr.at[dz], vr_sem.at[dz], zdev(1))
        elif dz < 0:
            d = -dz
            if d + 1 < far:
                arrived(r_vl.at[d + 1], vl_sem.at[d + 1])
                total = total + wide(r_vl.at[d + 1])
            s_vl[d] = total.astype(BF16)
            send(s_vl.at[d], r_vl.at[d], vl_sem.at[d], zdev(-1))
        else:
            arrived(r_vr.at[1], vr_sem.at[1])
            arrived(r_vl.at[1], vl_sem.at[1])
            dv_d[...] += total + wide(r_vr.at[1]) + wide(r_vl.at[1])

    for i, dz in enumerate(order):
        v_lo, v_hi = back_group(dz)
        p_v[i, :, 0:HALF] = v_lo.astype(BF16)
        p_v[i, :, HALF:LD] = v_hi.astype(BF16)
        give_v(i)
        if dz:
            pass_k(dz)
        if i >= 2:
            pass_v(i - 2)
        if i == 0:
            totals()
        if i == 3:
            totals_x()
    last = len(order) - 1
    for rows, keys in ((A, slice(0, HALF)), (B, slice(HALF, LD))):
        dk_own, dv_own = back(k_all[me, keys], v_all[me, keys], rows, tri)
        dk_d[keys], dv_d[keys] = dk_own * SCALE, dv_own
    pass_v(last - 1)
    for dx in OTHERS + (0,):
        xx = xi(dx)
        arrived(r_kr.at[1, xx], kr_sem.at[1, xx])
        arrived(r_kl.at[1, xx], kl_sem.at[1, xx])
        total = p_k[xx] + r_kr[1, xx].astype(F32) + r_kl[1, xx].astype(F32)
        if dx:
            s_kx[xx] = total.astype(BF16)
            send(s_kx.at[xx], r_kx.at[dx], kx_sem.at[dx], xdev(dx))
        else:
            dk_d[...] += total
    dq_ref[A], dq_ref[B] = ordered((dq_s[...] * SCALE).T)
    store(dq_ref, dq_hbm)
    pass_v(last)
    dv_ref[0:HALF], dv_ref[HALF:LD] = ordered(dv_d[...])
    store(dv_ref, dv_hbm)
    totals_z()
    for dx in OTHERS:
        arrived(r_kx.at[dx], kx_sem.at[dx])
    dk_d[...] += wide(r_kx.at[1]) + wide(r_kx.at[2]) + wide(r_kx.at[3])
    dk_ref[0:HALF], dk_ref[HALF:LD] = ordered(dk_d[...])
    store(dk_ref, dk_hbm)
    for copy in sends:
        copy.wait_send()
    for copy in stores:
        copy.wait()


def hand_over(*refs):
    ins, outs, held, (in_sem, out_sem) = refs[:5], refs[5:10], refs[10:15], refs[15:]
    first = [pltpu.make_async_copy(ins[i], held[i], in_sem.at[i]) for i in range(5)]
    second = [pltpu.make_async_copy(held[i], outs[i], out_sem.at[i]) for i in range(5)]
    for copy in first:
        copy.start()
    for one, two in zip(first, second):
        one.wait()
        two.start()
    for copy in second:
        copy.wait()


def local(nz, nh, queries, key_rows, value_rows, token_pos, step_len, label_count, out_grad, reward_weight):
    far, n = nz // 2, nz * NX
    hbm = pl.BlockSpec(memory_space=pltpu.HBM)
    block = (LD, HD)
    results = [((1, STEPS), F32), ((ROWS, HD), BF16), (block, BF16), (block, BF16), ((GROUP, HD), F32)]
    shapes = [jax.ShapeDtypeStruct(s, t) for s, t in results]
    scratch = results + [
        ((1, LD), jnp.int32), ((1, STEPS), jnp.int32), ((1, STEPS), jnp.int32), ((GROUP, HD), BF16),
        ((ROWS, HD), BF16), ((ROWS, HD), BF16), (block, BF16), (block, BF16),
        ((n, LD + META, HD), BF16), ((n,) + block, BF16),
        ((ROWS, HD), BF16), ((HD, ROWS), BF16), ((ROWS, HD), BF16), ((HD, ROWS), BF16), ((HD, ROWS), F32),
        ((1, ROWS), F32), ((1, ROWS), F32), ((HD, ROWS), F32), ((HD, ROWS), F32), ((1, ROWS), F32), ((1, ROWS), F32),
        ((ROWS, LD), BF16), ((LD, ROWS), BF16), ((STEPS, LD), F32),
        ((nh, 8, HD), F32), ((NX, 16, HD), F32), ((nz, 16, HD), F32),
    ]
    chain = ((far + 1, NX) + block, BF16)
    scratch += [chain] * 4 + [((NX,) + block, F32), ((NX,) + block, BF16), ((NX,) + block, BF16)]
    scratch += [((nz, NX) + block, BF16), ((nz, NX) + block, BF16)] + [((far + 1,) + block, BF16)] * 4
    scratch += [(block, F32), (block, F32)]
    dma = lambda *shape: pltpu.SemaphoreType.DMA(shape)
    sems = [
        dma(8), dma(5), dma(256), dma(n), dma(n), dma(nh), dma(NX), dma(nz),
        dma(far + 1, NX), dma(far + 1, NX), dma(NX), dma(nz, NX), dma(far + 1), dma(far + 1),
    ]
    partial = pl.pallas_call(
        functools.partial(kernel, nz, nh),
        out_shape=shapes,
        in_specs=[hbm] * 8,
        out_specs=[hbm] * 5,
        scratch_shapes=[pltpu.VMEM(s, t) for s, t in scratch] + sems,
        compiler_params=pltpu.CompilerParams(
            collective_id=0, has_side_effects=True, vmem_limit_bytes=VMEM_BYTES
        ),
    )(
        token_pos.reshape(1, LD),
        step_len.reshape(1, STEPS),
        label_count.reshape(1, STEPS),
        reward_weight,
        queries.reshape(ROWS, HD),
        out_grad.reshape(ROWS, HD),
        key_rows.reshape(block),
        value_rows.reshape(block),
    )
    loss, dq, dk, dv, dr = pl.pallas_call(
        hand_over,
        out_shape=shapes,
        in_specs=[hbm] * 5,
        out_specs=[hbm] * 5,
        scratch_shapes=[pltpu.VMEM(s, t) for s, t in results] + [dma(5), dma(5)],
        compiler_params=pltpu.CompilerParams(vmem_limit_bytes=VMEM_BYTES),
    )(*partial)
    return (
        loss.reshape(STEPS),
        dq.reshape(queries.shape),
        dk.reshape(key_rows.shape),
        dv.reshape(value_rows.shape),
        dr,
    )


def solution(mesh):
    rows = P(("dp", "ctx"), "head", None)
    return jax.shard_map(
        functools.partial(local, mesh.shape["ctx"] // NX, mesh.shape["head"]),
        mesh=mesh,
        in_specs=(rows, rows, rows, P(("dp", "ctx")), P("dp"), P("dp"), rows, P("head", None)),
        out_specs=(P("dp"), rows, rows, rows, P(("dp", "head"), None)),
        check_vma=False,
    )
```

time: 79.5 us -> 66.8 us (0.84)
  local copies, waits for them, and re-layouts: 7.12 us -> 0 us
  Pallas kernels: 70.9 us -> 65.8 us
    unnamed x21 -> x0, local copies, waits for them, and re-layouts: 7.12 us -> none
    pallas_call x1 -> x2, Pallas kernels: 70.9 us -> 65.8 us  [the longest x1 64 us: local(): pl.pallas_call(functools.partial(kernel, nz, nh), out_shape=shapes, in_sp...]
where the time goes in v2:
time: 66.8 us; the launch traced here: 66.6 us
  Pallas kernels  65.8 us (99%)
  between operations  0.8 us (1%)
    pallas_call x1, Pallas kernels, local(): pl.pallas_call(functools.partial(kernel, nz, nh), out_shape=shapes, in_sp...  64 us
    pallas_call x1, Pallas kernels, local(): pl.pallas_call(hand_over, out_shape=shapes, in_specs=[hbm] * 5, out_specs...  1.76 us

profile of v2, /device:TPU:2, one launch (start us, length us, event | category | flops | bytes accessed | tf_op | source)
XLA Modules:
  0.0 66.6 jit_solution(6213761775813327560)
XLA Ops:
  0.6 64.0 %shard_map.119 = (f32[1,64]{1,0:T(1,128)}, bf16[1024,128]{1,0:T(8,128)(2,1)}, bf16[128,128]{1,0:T(8,128)(2,1)}, bf16[128,128]{1,0:T(8,128)(2,1)}, f32[8,128]{1,0:T(8,128)}) custom-call(s32[1,128]{1,0:T(1,128)} %bitcast.15, s32[1,64]{1,0:T(1,128)} %bitcast.16, s32[1,64]{1,0:T(1,128)} %bitcast.17, bf16[8,128]{1,0:T(8,128)(2,1)} %rw_hbm.1, ...), custom_call_target="tpu_custom_call" | custom-call | tf_op jit(solution)/shard_map/pallas_call | solution.py:499
  64.7 1.8 %shard_map.120 = (f32[1,64]{1,0:T(1,128)}, bf16[1024,128]{1,0:T(8,128)(2,1)}, bf16[128,128]{1,0:T(8,128)(2,1)}, bf16[128,128]{1,0:T(8,128)(2,1)}, f32[8,128]{1,0:T(8,128)}) custom-call(f32[1,64]{1,0:T(1,128)} %get-tuple-element.15.refs_0_, bf16[1024,128]{1,0:T(8,128)(2,1)} %get-tuple-element.16.refs_1_, bf16[128,128]{1,0:T(8,128)(2,1)} %get-tuple-element.17.refs_2_, ...), custom_call_target="tpu_custom_call" | custom-call | tf_op jit(solution)/shard_map/pallas_call | solution.py:518

commit v3 on v2

--- a/solution.py
+++ b/solution.py
@@ -56,10 +56,9 @@
     loss_ref, dq_ref, dk_ref, dv_ref, dr_ref, pos_ref, step_ref, label_ref, rw_ref, q_ref, g_ref, k_ref, v_ref,
     k_all, v_all, qn, qt, gn, gt, rwt, top_s, tot_s, out_s, dq_s, lse_s, delta_s,
     to_tok, to_row, owned_s, hx, tx, tz,
-    s_kr, r_kr, s_kl, r_kl, p_k, s_kx, r_kx,
-    p_v, r_v, s_vr, r_vr, s_vl, r_vl, dk_d, dv_d,
+    held, p_k, s_k, r_k, s_kx, r_kx, p_v, r_v, s_v, r_v2, dk_d, dv_d,
     in_sem, out_sem, send_sem, k_sem, v_sem, h_sem, tx_sem, tz_sem,
-    kr_sem, kl_sem, kx_sem, rv_sem, vr_sem, vl_sem,
+    rk_sem, kx_sem, rv_sem, vz_sem,
 ):
     far = nz // 2
     me = lax.axis_index("ctx")
@@ -290,6 +289,22 @@
     hx[hd] = jnp.broadcast_to(score, (8, LD))
     for dh in range(1, nh):
         send(hx.at[hd], hx.at[hd], h_sem.at[hd], hdev(dh))
+    early = [far, far - 1, 1 - far]
+
+    def blocks(dz):
+        zz = zi(dz)
+        kl, ku, vl, vu = (keys_of(r, zz, h) for r in (k_all, v_all) for h in (0, 1))
+        return ((kl, vl, A, bias_of(zz, True)), (kl, vl, B, None), (ku, vu, B, bias_of(zz, False)))
+
+    def prob_of(k, rows, bias):
+        s = nn(k, qt[:, rows])
+        if bias is not None:
+            s = s + bias
+        return jnp.exp2(s * C2 - lse_s[:, rows])
+
+    for j, dz in enumerate(early):
+        for b, (k, _, rows, bias) in enumerate(blocks(dz)):
+            held[j, b] = prob_of(k, rows, bias)
     owned = owned_s[...]
     owned_low = owned.astype(BF16)
     target = label_ref[...].astype(F32) / ROLLOUTS
@@ -343,108 +358,127 @@
         store(dr_ref, dr_hbm)
         store(loss_ref, loss_hbm)
 
-    def back(k, v, rows, bias):
-        s = nn(k, qt[:, rows])
-        if bias is not None:
-            s = s + bias
-        p = jnp.exp2(s * C2 - lse_s[:, rows])
+    def back(k, v, rows, p):
         ds = (p * (nn(v, gt[:, rows]) - delta_s[:, rows])).astype(BF16)
         dq_s[:, rows] += tn(k, ds)
         return nn(ds, qn[rows]), nn(p.astype(BF16), gn[rows])
 
     def back_group(dz):
-        zz = zi(dz)
-        kl, ku, vl, vu = (keys_of(r, zz, h) for r in (k_all, v_all) for h in (0, 1))
-        k1, v1 = back(kl, vl, A, bias_of(zz, True))
-        k2, v2 = back(kl, vl, B, None)
-        k3, v3 = back(ku, vu, B, bias_of(zz, False))
-        p_k[:, 0:HALF] = ((k1 + k2) * SCALE).reshape(NX, HALF, HD)
-        p_k[:, HALF:LD] = (k3 * SCALE).reshape(NX, HALF, HD)
-        return (v1 + v2).reshape(NX, HALF, HD), v3.reshape(NX, HALF, HD)
+        (k1, v1), (k2, v2), (k3, v3) = (
+            back(k, v, rows, held[early.index(dz), b] if dz in early else prob_of(k, rows, bias))
+            for b, (k, v, rows, bias) in enumerate(blocks(dz))
+        )
+        whole = (NX, HALF, HD)
+        return ((k1 + k2) * SCALE).reshape(whole), (k3 * SCALE).reshape(whole), (v1 + v2).reshape(whole), v3.reshape(whole)
 
     def wide(ref):
         return ref[...].astype(F32)
 
-    order = [far]
-    for s in range(far - 1, 0, -1):
-        order += [s, -s]
-    order += [0]
-    two = NX // 2
-
-    def pass_k(dz):
-        d = abs(dz)
-        for xx in range(NX):
-            for right in (True, False):
-                crosses = (xx < two) == right
-                if (dz == far and not crosses) or (dz != far and (dz > 0) != right):
+    FAR, THREE, MID, ONE, OWN = range(5)
+    turns = (2,) + tuple(d for d in OTHERS if d != 2) + (0,)
+
+    def comes(level, w, j):
+        return level != FAR or (j < NX // 2) == (w == 0)
+
+    def to_owner(level, ways, add=None):
+        for j, dx in enumerate(turns):
+            for w in ways:
+                if not comes(level, w, j):
                     continue
-                s_k, r_k, sem = (s_kr, r_kr, kr_sem) if right else (s_kl, r_kl, kl_sem)
-                own = p_k[xx]
-                if d + 1 < far or (d + 1 == far and crosses):
-                    arrived(r_k.at[d + 1, xx], sem.at[d + 1, xx])
-                    own = own + wide(r_k.at[d + 1, xx])
-                s_k[d, xx] = own.astype(BF16)
-                send(s_k.at[d, xx], r_k.at[d, xx], sem.at[d, xx], zdev(1 if right else -1))
-
-    def give_v(i):
+                total = p_k[level, 0 if level == FAR else w, xi(dx)]
+                for other in add or ():
+                    if comes(other, w, j):
+                        total = total + got_k(other, w, j)
+                s_k[level, w, j] = total.astype(BF16)
+                hops = 2 if level == FAR else 1
+                send(s_k.at[level, w, j], r_k.at[level, w, j], rk_sem.at[level, w, j], zdev(-hops if w else hops))
+
+    def got_k(level, w, j):
+        arrived(r_k.at[level, w, j], rk_sem.at[level, w, j])
+        return wide(r_k.at[level, w, j])
+
+    def give_v(level):
         for dx in OTHERS:
-            send(p_v.at[i, xi(dx)], r_v.at[i, dx], rv_sem.at[i, dx], xdev(dx))
-
-    def pass_v(i):
-        dz = order[i]
-        total = p_v[i, x].astype(F32)
+            if level in (FAR, OWN):
+                send(p_v.at[level, xi(dx), 0], r_v.at[level, dx, 0], rv_sem.at[level, dx], xdev(dx))
+            else:
+                send(p_v.at[level, xi(dx)], r_v.at[level, dx], rv_sem.at[level, dx], xdev(dx))
+
+    def sum_v(level):
+        one = level in (FAR, OWN)
+        total = p_v[level, x, 0].astype(F32) if one else p_v[level, x].astype(F32)
         for dx in OTHERS:
-            arrived(r_v.at[i, dx], rv_sem.at[i, dx])
-            total = total + wide(r_v.at[i, dx])
-        if dz > 0:
-            if dz < far:
-                arrived(r_vr.at[dz + 1], vr_sem.at[dz + 1])
-                total = total + wide(r_vr.at[dz + 1])
-            s_vr[dz] = total.astype(BF16)
-            send(s_vr.at[dz], r_vr.at[dz], vr_sem.at[dz], zdev(1))
-        elif dz < 0:
-            d = -dz
-            if d + 1 < far:
-                arrived(r_vl.at[d + 1], vl_sem.at[d + 1])
-                total = total + wide(r_vl.at[d + 1])
-            s_vl[d] = total.astype(BF16)
-            send(s_vl.at[d], r_vl.at[d], vl_sem.at[d], zdev(-1))
-        else:
-            arrived(r_vr.at[1], vr_sem.at[1])
-            arrived(r_vl.at[1], vl_sem.at[1])
-            dv_d[...] += total + wide(r_vr.at[1]) + wide(r_vl.at[1])
-
-    for i, dz in enumerate(order):
-        v_lo, v_hi = back_group(dz)
-        p_v[i, :, 0:HALF] = v_lo.astype(BF16)
-        p_v[i, :, HALF:LD] = v_hi.astype(BF16)
-        give_v(i)
-        if dz:
-            pass_k(dz)
-        if i >= 2:
-            pass_v(i - 2)
-        if i == 0:
-            totals()
-        if i == 3:
-            totals_x()
-    last = len(order) - 1
+            ref = r_v.at[level, dx, 0] if one else r_v.at[level, dx]
+            arrived(ref, rv_sem.at[level, dx])
+            total = total + wide(ref)
+        return total
+
+    def got_v(level, w):
+        arrived(r_v2.at[level, w], vz_sem.at[level, w])
+        return wide(r_v2.at[level, w])
+
+    def pass_v(level):
+        total = sum_v(level)
+        if level == FAR:
+            s_v[FAR, 0] = total.astype(BF16)
+            send(s_v.at[FAR, 0], r_v2.at[FAR, 0], vz_sem.at[FAR, 0], zdev(2))
+            return
+        right, left = total[0], total[1]
+        if level == MID:
+            right = right + got_v(THREE, 0) + got_v(FAR, 0)
+            left = left + got_v(THREE, 1)
+        if level == ONE:
+            right, left = right + got_v(MID, 0), left + got_v(MID, 1)
+        for w, value in ((0, right), (1, left)):
+            s_v[level, w] = value.astype(BF16)
+            send(s_v.at[level, w], r_v2.at[level, w], vz_sem.at[level, w], zdev(-1 if w else 1))
+
+    def group(level, right=True):
+        dz = {FAR: far, THREE: 3, MID: 2, ONE: 1, OWN: 0}[level] * (1 if right else -1)
+        w = 0 if right else 1
+        k_lo, k_hi, v_lo, v_hi = back_group(dz)
+        p_v[level, :, w, 0:HALF] = v_lo.astype(BF16)
+        p_v[level, :, w, HALF:LD] = v_hi.astype(BF16)
+        p_k[level, w, :, 0:HALF], p_k[level, w, :, HALF:LD] = k_lo, k_hi
+
+    group(FAR)
+    to_owner(FAR, (0, 1))
+    give_v(FAR)
+    group(THREE)
+    to_owner(THREE, (0,))
+    group(THREE, False)
+    to_owner(THREE, (1,))
+    give_v(THREE)
+    group(MID)
+    group(MID, False)
+    give_v(MID)
+    pass_v(FAR)
+    to_owner(MID, (0, 1), (THREE, FAR))
+    group(ONE)
+    totals()
+    pass_v(THREE)
+    group(ONE, False)
+    give_v(ONE)
+    to_owner(ONE, (0, 1), (MID,))
+    group(OWN)
+    give_v(OWN)
+    totals_x()
+    pass_v(MID)
     for rows, keys in ((A, slice(0, HALF)), (B, slice(HALF, LD))):
-        dk_own, dv_own = back(k_all[me, keys], v_all[me, keys], rows, tri)
+        k_own = k_all[me, keys]
+        dk_own, dv_own = back(k_own, v_all[me, keys], rows, prob_of(k_own, rows, tri))
         dk_d[keys], dv_d[keys] = dk_own * SCALE, dv_own
-    pass_v(last - 1)
-    for dx in OTHERS + (0,):
-        xx = xi(dx)
-        arrived(r_kr.at[1, xx], kr_sem.at[1, xx])
-        arrived(r_kl.at[1, xx], kl_sem.at[1, xx])
-        total = p_k[xx] + r_kr[1, xx].astype(F32) + r_kl[1, xx].astype(F32)
+    pass_v(ONE)
+    for j, dx in enumerate(turns):
+        total = p_k[OWN, 0, xi(dx)] + got_k(ONE, 0, j) + got_k(ONE, 1, j)
         if dx:
-            s_kx[xx] = total.astype(BF16)
-            send(s_kx.at[xx], r_kx.at[dx], kx_sem.at[dx], xdev(dx))
+            s_kx[dx] = total.astype(BF16)
+            send(s_kx.at[dx], r_kx.at[dx], kx_sem.at[dx], xdev(dx))
         else:
             dk_d[...] += total
     dq_ref[A], dq_ref[B] = ordered((dq_s[...] * SCALE).T)
     store(dq_ref, dq_hbm)
-    pass_v(last)
+    dv_d[...] += sum_v(OWN) + got_v(ONE, 0) + got_v(ONE, 1)
     dv_ref[0:HALF], dv_ref[HALF:LD] = ordered(dv_d[...])
     store(dv_ref, dv_hbm)
     totals_z()
@@ -473,7 +507,7 @@
 
 
 def local(nz, nh, queries, key_rows, value_rows, token_pos, step_len, label_count, out_grad, reward_weight):
-    far, n = nz // 2, nz * NX
+    n = nz * NX
     hbm = pl.BlockSpec(memory_space=pltpu.HBM)
     block = (LD, HD)
     results = [((1, STEPS), F32), ((ROWS, HD), BF16), (block, BF16), (block, BF16), ((GROUP, HD), F32)]
@@ -487,14 +521,17 @@
         ((ROWS, LD), BF16), ((LD, ROWS), BF16), ((STEPS, LD), F32),
         ((nh, 8, HD), F32), ((NX, 16, HD), F32), ((nz, 16, HD), F32),
     ]
-    chain = ((far + 1, NX) + block, BF16)
-    scratch += [chain] * 4 + [((NX,) + block, F32), ((NX,) + block, BF16), ((NX,) + block, BF16)]
-    scratch += [((nz, NX) + block, BF16), ((nz, NX) + block, BF16)] + [((far + 1,) + block, BF16)] * 4
+    four = (NX,) + block
+    scratch += [
+        ((3, 3, NX * HALF, RHALF), F32), ((5, 2) + four, F32),
+        ((4, 2) + four, BF16), ((4, 2) + four, BF16), (four, BF16), (four, BF16),
+        ((5, NX, 2) + block, BF16), ((5, NX, 2) + block, BF16), ((4, 2) + block, BF16), ((4, 2) + block, BF16),
+    ]
     scratch += [(block, F32), (block, F32)]
     dma = lambda *shape: pltpu.SemaphoreType.DMA(shape)
     sems = [
         dma(8), dma(5), dma(256), dma(n), dma(n), dma(nh), dma(NX), dma(nz),
-        dma(far + 1, NX), dma(far + 1, NX), dma(NX), dma(nz, NX), dma(far + 1), dma(far + 1),
+        dma(4, 2, NX), dma(NX), dma(5, NX), dma(4, 2),
     ]
     partial = pl.pallas_call(
         functools.partial(kernel, nz, nh),

time: 66.8 us -> 65.5 us (0.981)
  Pallas kernels: 65.8 us -> 64.5 us
    pallas_call x1, Pallas kernels: 64 us -> 62.8 us  [local(): pl.pallas_call(functools.partial(kernel, nz, nh), out_shape=shapes, in_sp...]
where the time goes in v3:
time: 65.5 us; the launch traced here: 65.3 us
  Pallas kernels  64.5 us (98%)
  between operations  0.8 us (1%)
    pallas_call x1, Pallas kernels, local(): pl.pallas_call(functools.partial(kernel, nz, nh), out_shape=shapes, in_sp...  62.8 us
    pallas_call x1, Pallas kernels, local(): pl.pallas_call(hand_over, out_shape=shapes, in_specs=[hbm] * 5, out_specs...  1.76 us

profile of v3, /device:TPU:2, one launch (start us, length us, event | category | flops | bytes accessed | tf_op | source)
XLA Modules:
  0.0 65.3 jit_solution(10696705902258051223)
XLA Ops:
  0.6 62.8 %shard_map.119 = (f32[1,64]{1,0:T(1,128)}, bf16[1024,128]{1,0:T(8,128)(2,1)}, bf16[128,128]{1,0:T(8,128)(2,1)}, bf16[128,128]{1,0:T(8,128)(2,1)}, f32[8,128]{1,0:T(8,128)}) custom-call(s32[1,128]{1,0:T(1,128)} %bitcast.15, s32[1,64]{1,0:T(1,128)} %bitcast.16, s32[1,64]{1,0:T(1,128)} %bitcast.17, bf16[8,128]{1,0:T(8,128)(2,1)} %rw_hbm.1, ...), custom_call_target="tpu_custom_call" | custom-call | tf_op jit(solution)/shard_map/pallas_call | solution.py:536
  63.4 1.8 %shard_map.120 = (f32[1,64]{1,0:T(1,128)}, bf16[1024,128]{1,0:T(8,128)(2,1)}, bf16[128,128]{1,0:T(8,128)(2,1)}, bf16[128,128]{1,0:T(8,128)(2,1)}, f32[8,128]{1,0:T(8,128)}) custom-call(f32[1,64]{1,0:T(1,128)} %get-tuple-element.15.refs_0_, bf16[1024,128]{1,0:T(8,128)(2,1)} %get-tuple-element.16.refs_1_, bf16[128,128]{1,0:T(8,128)(2,1)} %get-tuple-element.17.refs_2_, ...), custom_call_target="tpu_custom_call" | custom-call | tf_op jit(solution)/shard_map/pallas_call | solution.py:555

commit v4 on v3

--- a/solution.py
+++ b/solution.py
@@ -110,18 +110,20 @@
     def send_v(at, dev):
         send(v_all.at[at], v_all.at[at], v_sem.at[at], dev)
 
-    barrier = pltpu.get_barrier_semaphore()
-    peers = [xdev(d) for d in range(1, NX)] + [zdev(d) for d in range(1, nz)] + [hdev(d) for d in range(1, nh)]
-    for dev in peers:
-        pl.semaphore_signal(barrier, inc=1, device_id=dev, device_id_type=MESH)
     pairs = [
         (pos_hbm, pos_ref), (k_hbm, k_ref), (v_hbm, v_ref), (q_hbm, q_ref), (g_hbm, g_ref),
         (rw_hbm, rw_ref), (step_hbm, step_ref), (label_hbm, label_ref),
     ]
     loads = [pltpu.make_async_copy(src, dst, in_sem.at[i]) for i, (src, dst) in enumerate(pairs)]
-    for load in loads:
+    for load in loads[0:3]:
         load.start()
 
+    barrier = pltpu.get_barrier_semaphore()
+    peers = [xdev(d) for d in range(1, NX)] + [zdev(d) for d in range(1, nz)] + [hdev(d) for d in range(1, nh)]
+    for dev in peers:
+        pl.semaphore_signal(barrier, inc=1, device_id=dev, device_id_type=MESH)
+    for load in loads[3:]:
+        load.start()
     for load in loads[0:3]:
         load.wait()
     pos = pos_ref[...].astype(F32)
@@ -289,7 +291,7 @@
     hx[hd] = jnp.broadcast_to(score, (8, LD))
     for dh in range(1, nh):
         send(hx.at[hd], hx.at[hd], h_sem.at[hd], hdev(dh))
-    early = [far, far - 1, 1 - far]
+    early = [far, far - 1, 1 - far, far - 2, 2 - far]
 
     def blocks(dz):
         zz = zi(dz)
@@ -460,10 +462,10 @@
     group(ONE, False)
     give_v(ONE)
     to_owner(ONE, (0, 1), (MID,))
+    pass_v(MID)
     group(OWN)
     give_v(OWN)
     totals_x()
-    pass_v(MID)
     for rows, keys in ((A, slice(0, HALF)), (B, slice(HALF, LD))):
         k_own = k_all[me, keys]
         dk_own, dv_own = back(k_own, v_all[me, keys], rows, prob_of(k_own, rows, tri))
@@ -482,13 +484,13 @@
     dv_ref[0:HALF], dv_ref[HALF:LD] = ordered(dv_d[...])
     store(dv_ref, dv_hbm)
     totals_z()
+    for copy in sends:
+        copy.wait_send()
     for dx in OTHERS:
         arrived(r_kx.at[dx], kx_sem.at[dx])
     dk_d[...] += wide(r_kx.at[1]) + wide(r_kx.at[2]) + wide(r_kx.at[3])
     dk_ref[0:HALF], dk_ref[HALF:LD] = ordered(dk_d[...])
     store(dk_ref, dk_hbm)
-    for copy in sends:
-        copy.wait_send()
     for copy in stores:
         copy.wait()
 
@@ -523,7 +525,7 @@
     ]
     four = (NX,) + block
     scratch += [
-        ((3, 3, NX * HALF, RHALF), F32), ((5, 2) + four, F32),
+        ((5, 3, NX * HALF, RHALF), F32), ((5, 2) + four, F32),
         ((4, 2) + four, BF16), ((4, 2) + four, BF16), (four, BF16), (four, BF16),
         ((5, NX, 2) + block, BF16), ((5, NX, 2) + block, BF16), ((4, 2) + block, BF16), ((4, 2) + block, BF16),
     ]

time: 65.5 us -> 65.1 us (level)
  no operation moved by 1% of the time
where the time goes in v4:
time: 65.1 us; the launch traced here: 65 us
  Pallas kernels  64.2 us (99%)
  between operations  0.8 us (1%)
    pallas_call x1, Pallas kernels, local(): pl.pallas_call(functools.partial(kernel, nz, nh), out_shape=shapes, in_sp...  62.4 us
    pallas_call x1, Pallas kernels, local(): pl.pallas_call(hand_over, out_shape=shapes, in_specs=[hbm] * 5, out_specs...  1.76 us

profile of v4, /device:TPU:2, one launch (start us, length us, event | category | flops | bytes accessed | tf_op | source)
XLA Modules:
  0.0 65.0 jit_solution(12583909001754968688)
XLA Ops:
  0.6 62.4 %shard_map.119 = (f32[1,64]{1,0:T(1,128)}, bf16[1024,128]{1,0:T(8,128)(2,1)}, bf16[128,128]{1,0:T(8,128)(2,1)}, bf16[128,128]{1,0:T(8,128)(2,1)}, f32[8,128]{1,0:T(8,128)}) custom-call(s32[1,128]{1,0:T(1,128)} %bitcast.15, s32[1,64]{1,0:T(1,128)} %bitcast.16, s32[1,64]{1,0:T(1,128)} %bitcast.17, bf16[8,128]{1,0:T(8,128)(2,1)} %rw_hbm.1, ...), custom_call_target="tpu_custom_call" | custom-call | tf_op jit(solution)/shard_map/pallas_call | solution.py:538
  63.0 1.8 %shard_map.120 = (f32[1,64]{1,0:T(1,128)}, bf16[1024,128]{1,0:T(8,128)(2,1)}, bf16[128,128]{1,0:T(8,128)(2,1)}, bf16[128,128]{1,0:T(8,128)(2,1)}, f32[8,128]{1,0:T(8,128)}) custom-call(f32[1,64]{1,0:T(1,128)} %get-tuple-element.15.refs_0_, bf16[1024,128]{1,0:T(8,128)(2,1)} %get-tuple-element.16.refs_1_, bf16[128,128]{1,0:T(8,128)(2,1)} %get-tuple-element.17.refs_2_, ...), custom_call_target="tpu_custom_call" | custom-call | tf_op jit(solution)/shard_map/pallas_call | solution.py:557

commit v5 on v4

--- a/solution.py
+++ b/solution.py
@@ -26,6 +26,7 @@
 NEG = -1e30
 A, B = slice(0, RHALF), slice(RHALF, ROWS)
 VMEM_BYTES = 60 * 2**20
+PIECES = 4
 OTHERS = (1, 3, 2)
 
 
@@ -415,20 +416,22 @@
             total = total + wide(ref)
         return total
 
-    def got_v(level, w):
-        arrived(r_v2.at[level, w], vz_sem.at[level, w])
-        return wide(r_v2.at[level, w])
+    def got_v(level, w, part=slice(0, LD)):
+        arrived(r_v2.at[level, w, part], vz_sem.at[level, w])
+        return wide(r_v2.at[level, w, part])
 
     def pass_v(level):
         total = sum_v(level)
         if level == FAR:
-            s_v[FAR, 0] = total.astype(BF16)
-            send(s_v.at[FAR, 0], r_v2.at[FAR, 0], vz_sem.at[FAR, 0], zdev(2))
+            for w, part in ((0, slice(0, HALF)), (1, slice(HALF, LD))):
+                s_v[FAR, w, part] = total[part].astype(BF16)
+                send(s_v.at[FAR, w, part], r_v2.at[FAR, w, part], vz_sem.at[FAR, w], zdev(-2 if w else 2))
             return
         right, left = total[0], total[1]
         if level == MID:
-            right = right + got_v(THREE, 0) + got_v(FAR, 0)
-            left = left + got_v(THREE, 1)
+            right, left = right + got_v(THREE, 0), left + got_v(THREE, 1)
+            right = jnp.concatenate([right[:HALF] + got_v(FAR, 0, slice(0, HALF)), right[HALF:]], axis=0)
+            left = jnp.concatenate([left[:HALF], left[HALF:] + got_v(FAR, 1, slice(HALF, LD))], axis=0)
         if level == ONE:
             right, left = right + got_v(MID, 0), left + got_v(MID, 1)
         for w, value in ((0, right), (1, left)):
@@ -497,8 +500,12 @@
 
 def hand_over(*refs):
     ins, outs, held, (in_sem, out_sem) = refs[:5], refs[5:10], refs[10:15], refs[15:]
-    first = [pltpu.make_async_copy(ins[i], held[i], in_sem.at[i]) for i in range(5)]
-    second = [pltpu.make_async_copy(held[i], outs[i], out_sem.at[i]) for i in range(5)]
+    piece = ROWS // PIECES
+    parts = [(1, pl.ds(p * piece, piece)) for p in range(PIECES)] + [(i, slice(None)) for i in (0, 2, 3, 4)]
+    first, second = [], []
+    for n, (i, at) in enumerate(parts):
+        first.append(pltpu.make_async_copy(ins[i].at[at], held[i].at[at], in_sem.at[n]))
+        second.append(pltpu.make_async_copy(held[i].at[at], outs[i].at[at], out_sem.at[n]))
     for copy in first:
         copy.start()
     for one, two in zip(first, second):
@@ -559,7 +566,7 @@
         out_shape=shapes,
         in_specs=[hbm] * 5,
         out_specs=[hbm] * 5,
-        scratch_shapes=[pltpu.VMEM(s, t) for s, t in results] + [dma(5), dma(5)],
+        scratch_shapes=[pltpu.VMEM(s, t) for s, t in results] + [dma(PIECES + 4), dma(PIECES + 4)],
         compiler_params=pltpu.CompilerParams(vmem_limit_bytes=VMEM_BYTES),
     )(*partial)
     return (

time: 65.1 us -> 65.1 us (level)
  no operation moved by 1% of the time
where the time goes in v5:
time: 65.1 us; the launch traced here: 64.9 us
  Pallas kernels  64.1 us (98%)
  between operations  0.8 us (1%)
    pallas_call x1, Pallas kernels, local(): pl.pallas_call(functools.partial(kernel, nz, nh), out_shape=shapes, in_sp...  62.4 us
    pallas_call x1, Pallas kernels, local(): pl.pallas_call(hand_over, out_shape=shapes, in_specs=[hbm] * 5, out_specs...  1.73 us

profile of v5, /device:TPU:2, one launch (start us, length us, event | category | flops | bytes accessed | tf_op | source)
XLA Modules:
  0.0 64.9 jit_solution(5887065379189805158)
XLA Ops:
  0.6 62.4 %shard_map.119 = (f32[1,64]{1,0:T(1,128)}, bf16[1024,128]{1,0:T(8,128)(2,1)}, bf16[128,128]{1,0:T(8,128)(2,1)}, bf16[128,128]{1,0:T(8,128)(2,1)}, f32[8,128]{1,0:T(8,128)}) custom-call(s32[1,128]{1,0:T(1,128)} %bitcast.15, s32[1,64]{1,0:T(1,128)} %bitcast.16, s32[1,64]{1,0:T(1,128)} %bitcast.17, bf16[8,128]{1,0:T(8,128)(2,1)} %rw_hbm.1, ...), custom_call_target="tpu_custom_call" | custom-call | tf_op jit(solution)/shard_map/pallas_call | solution.py:545
  63.0 1.7 %shard_map.120 = (f32[1,64]{1,0:T(1,128)}, bf16[1024,128]{1,0:T(8,128)(2,1)}, bf16[128,128]{1,0:T(8,128)(2,1)}, bf16[128,128]{1,0:T(8,128)(2,1)}, f32[8,128]{1,0:T(8,128)}) custom-call(f32[1,64]{1,0:T(1,128)} %get-tuple-element.15.refs_0_, bf16[1024,128]{1,0:T(8,128)(2,1)} %get-tuple-element.16.refs_1_, bf16[128,128]{1,0:T(8,128)(2,1)} %get-tuple-element.17.refs_2_, ...), custom_call_target="tpu_custom_call" | custom-call | tf_op jit(solution)/shard_map/pallas_call | solution.py:564

commit v6 on v4

--- a/solution.py
+++ b/solution.py
@@ -26,7 +26,7 @@
 NEG = -1e30
 A, B = slice(0, RHALF), slice(RHALF, ROWS)
 VMEM_BYTES = 60 * 2**20
-OTHERS = (1, 3, 2)
+OTHERS = (2, 1, 3)
 
 
 def nn(a, b):

time: 65.1 us -> 65.2 us (level)
  no operation moved by 1% of the time
where the time goes in v6:
time: 65.2 us; the launch traced here: 65 us
  Pallas kernels  64.2 us (98%)
  between operations  0.8 us (1%)
    pallas_call x1, Pallas kernels, local(): pl.pallas_call(functools.partial(kernel, nz, nh), out_shape=shapes, in_sp...  62.5 us
    pallas_call x1, Pallas kernels, local(): pl.pallas_call(hand_over, out_shape=shapes, in_specs=[hbm] * 5, out_specs...  1.76 us

profile of v6, /device:TPU:2, one launch (start us, length us, event | category | flops | bytes accessed | tf_op | source)
XLA Modules:
  0.0 65.0 jit_solution(10185385960092751583)
XLA Ops:
  0.6 62.5 %shard_map.119 = (f32[1,64]{1,0:T(1,128)}, bf16[1024,128]{1,0:T(8,128)(2,1)}, bf16[128,128]{1,0:T(8,128)(2,1)}, bf16[128,128]{1,0:T(8,128)(2,1)}, f32[8,128]{1,0:T(8,128)}) custom-call(s32[1,128]{1,0:T(1,128)} %bitcast.15, s32[1,64]{1,0:T(1,128)} %bitcast.16, s32[1,64]{1,0:T(1,128)} %bitcast.17, bf16[8,128]{1,0:T(8,128)(2,1)} %rw_hbm.1, ...), custom_call_target="tpu_custom_call" | custom-call | tf_op jit(solution)/shard_map/pallas_call | solution.py:538
  63.1 1.8 %shard_map.120 = (f32[1,64]{1,0:T(1,128)}, bf16[1024,128]{1,0:T(8,128)(2,1)}, bf16[128,128]{1,0:T(8,128)(2,1)}, bf16[128,128]{1,0:T(8,128)(2,1)}, f32[8,128]{1,0:T(8,128)}) custom-call(f32[1,64]{1,0:T(1,128)} %get-tuple-element.15.refs_0_, bf16[1024,128]{1,0:T(8,128)(2,1)} %get-tuple-element.16.refs_1_, bf16[128,128]{1,0:T(8,128)(2,1)} %get-tuple-element.17.refs_2_, ...), custom_call_target="tpu_custom_call" | custom-call | tf_op jit(solution)/shard_map/pallas_call | solution.py:557
